TPU v7x, 128 devices: a whole 4x4x4 slice. The times are simulated.
128 devices in a mesh: tok: 32 (over x, z, core), head: 4 (over y).
Axes of the slice: x: 4, y: 4, z: 4, core: 2. Of those that a mesh axis runs over, the one named last changes fastest.
Arguments:
- activations: bfloat16 [8192, 2048], P('tok'), may hold values from -6 to 6
- labels: int32 [8192], P('tok'), may hold values from 0 to 2
- position: int32 [8192], P('tok'), may hold values from 0 to 8191, as said below
- norm_gains: float32 [6, 2048], replicated, may hold values from 0.1 to 1.9
- qkv_weight: bfloat16 [2048, 3, 2048], P(None, None, 'head'), may hold values from -0.125 to 0.125
- out_weight: bfloat16 [2048, 2048], P('head'), may hold values from -0.75 to 0.75
- up_weight: bfloat16 [2048, 8192], P(None, 'head'), may hold values from -0.125 to 0.125
- down_weight: bfloat16 [8192, 2048], P('head'), may hold values from -0.09375 to 0.09375
- cotangent: bfloat16 [8192, 2048], P('tok'), may hold values from -6 to 6
Outputs:
- layer_out: bfloat16 [8192, 2048], P('tok')
- grad_input: float32 [8192, 2048], P('tok')
- grad_gains: float32 [6, 2048], P(None, 'tok')
- grad_qkv: float32 [2048, 3, 2048], P('tok', None, 'head')
- grad_out: float32 [2048, 2048], P(('head', 'tok'))
- grad_up: float32 [2048, 8192], P('tok', 'head')
- grad_down: float32 [8192, 2048], P(('head', 'tok'))
Inputs may be any that keep to these rules, and one draw needn't show every extreme that they name: position is a permutation of the 8192 places. Of the 256 rows of one device at most 16 have places in any one block of 256 consecutive places, and every device has exactly 16 in some block.
All inputs are finite; a program needn't handle non-finite values.
Results may differ from a plain program's by a relative error of at most 0.03.
Values may be sent and summed in bfloat16 or wider, within the bound.
A program may use at most 320 MiB of HBM per device.

v0:
```python
import math

import jax
import jax.numpy as jnp
from jax import lax
from jax.sharding import PartitionSpec as P

HD = 128


highest = lax.Precision.HIGHEST


def layer_norm(values_in):
    row_mean = jnp.mean(values_in, axis=-1, keepdims=True)
    centred = values_in - row_mean
    inverse = lax.rsqrt(jnp.mean(centred * centred, axis=-1, keepdims=True) + 1e-05)
    return (centred * inverse, inverse)


def norm_back(grad_in, normed, inverse):
    return inverse * (
        grad_in
        - jnp.mean(grad_in, axis=-1, keepdims=True)
        - normed * jnp.mean(grad_in * normed, axis=-1, keepdims=True)
    )


def tables(place_now, head_dim):
    half_dim = head_dim // 2
    frequency = jnp.exp(
        jnp.arange(half_dim, dtype=jnp.float32) * (-2.0 * math.log(10000.0) / head_dim)
    )
    angles = place_now.astype(jnp.float32)[:, None] * frequency[None, :]
    angles = jnp.concatenate([angles, angles], axis=-1)
    return (jnp.cos(angles), jnp.sin(angles))


def rotate(values_in, cosine, sine):
    half_dim = values_in.shape[-1] // 2
    turned = jnp.concatenate([-values_in[..., half_dim:], values_in[..., :half_dim]], axis=-1)
    return values_in * cosine[:, None, :] + turned * sine[:, None, :]


def rotate_back(grad_in, cosine, sine):
    half_dim = grad_in.shape[-1] // 2
    scaled = grad_in * sine[:, None, :]
    return grad_in * cosine[:, None, :] + jnp.concatenate(
        [scaled[..., half_dim:], -scaled[..., :half_dim]], axis=-1
    )


def clip_place(device, row_in, tok_rows, first_rows):
    second = row_in >= first_rows
    place_now = jnp.where(
        second, device * (tok_rows - first_rows) + row_in - first_rows, device * first_rows + row_in
    )
    return (second, place_now)


def per_device(
    activations,
    labels,
    position,
    norm_gains,
    qkv_weight,
    out_weight,
    up_weight,
    down_weight,
    cotangent,
):
    tok_rows, width = activations.shape
    mode_count = norm_gains.shape[0] // 2
    local_width = qkv_weight.shape[2]
    heads_here = local_width // HD
    peer_count = lax.axis_size("tok")
    capacity = 2 * tok_rows // peer_count
    first_rows = 3 * tok_rows // 4
    score_scale = HD ** (-0.5)
    residual = activations.astype(jnp.float32)
    onehot = (labels[:, None] == jnp.arange(mode_count, dtype=jnp.int32)[None, :]).astype(
        jnp.float32
    )
    gain_one = jnp.dot(onehot, norm_gains[:mode_count], precision=highest)
    gain_two = jnp.dot(onehot, norm_gains[mode_count:], precision=highest)
    normed_one, inverse_one = layer_norm(residual)
    input_one = (normed_one * gain_one).astype(jnp.bfloat16)
    target_dev = position // tok_rows
    target_row = position % tok_rows
    unused_clip, target_place = clip_place(target_dev, target_row, tok_rows, first_rows)
    cosine, sine = tables(target_place, HD)
    projected = jnp.einsum("td,dkh->tkh", input_one, qkv_weight, preferred_element_type=jnp.float32)
    query_rot = rotate(projected[:, 0].reshape(tok_rows, heads_here, HD), cosine, sine)
    key_rot = rotate(projected[:, 1].reshape(tok_rows, heads_here, HD), cosine, sine)
    packed = jnp.stack(
        [
            query_rot.reshape(tok_rows, local_width),
            key_rot.reshape(tok_rows, local_width),
            projected[:, 2],
        ],
        axis=1,
    ).astype(jnp.bfloat16)
    choose = (target_dev[:, None] == jnp.arange(peer_count, dtype=jnp.int32)[None, :]).astype(
        jnp.int32
    )
    before = jnp.cumsum(choose, axis=0) - choose
    send_slot = target_dev * capacity + jnp.sum(before * choose, axis=1)
    send_rows = jnp.full((peer_count * capacity,), -1, jnp.int32).at[send_slot].set(target_row)
    came_rows = lax.all_to_all(
        send_rows.reshape(peer_count, capacity), "tok", split_axis=0, concat_axis=0, tiled=True
    ).reshape(-1)
    from_slot = (
        jnp.zeros((tok_rows,), jnp.int32)
        .at[jnp.where(came_rows >= 0, came_rows, tok_rows)]
        .set(jnp.arange(peer_count * capacity, dtype=jnp.int32), mode="drop")
    )
    outgoing = (
        jnp.zeros((peer_count * capacity, 3, local_width), jnp.bfloat16).at[send_slot].set(packed)
    )
    arrived = lax.all_to_all(
        outgoing.reshape(peer_count, capacity, 3, local_width),
        "tok",
        split_axis=0,
        concat_axis=0,
        tiled=True,
    ).reshape(peer_count * capacity, 3, local_width)[from_slot]
    own_index = lax.axis_index("tok")
    own_second, own_place = clip_place(
        own_index, jnp.arange(tok_rows, dtype=jnp.int32), tok_rows, first_rows
    )
    queries = arrived[:, 0].reshape(tok_rows, heads_here, HD)
    keys_values = arrived[:, 1:]

    def key_mask(key_count):
        global_rows = jnp.arange(key_count, dtype=jnp.int32)
        key_second, key_place = clip_place(
            global_rows // tok_rows, global_rows % tok_rows, tok_rows, first_rows
        )
        return (own_second[:, None] == key_second[None, :]) & (
            key_place[None, :] <= own_place[:, None]
        )

    def piece_scores(kv_piece):
        key_count = kv_piece.shape[0]
        key_heads = kv_piece[:, 0].reshape(key_count, heads_here, HD)
        value_heads = kv_piece[:, 1].reshape(key_count, heads_here, HD)
        scores = (
            jnp.einsum("qhd,khd->hqk", queries, key_heads, preferred_element_type=jnp.float32)
            * score_scale
        )
        scores = jnp.where(key_mask(key_count)[None], scores, -1e30)
        return (scores, key_heads, value_heads)

    def over_keys(step_fn, initial):
        result_now = step_fn(
            initial, lax.all_gather(keys_values, "tok", axis=0, tiled=True), jnp.int32(0)
        )
        return result_now

    def normalizer_piece(state_now, kv_piece, row_start):
        running_max, running_sum = state_now
        scores, key_heads, value_heads = piece_scores(kv_piece)
        new_max = jnp.maximum(running_max, jnp.max(scores, axis=-1))
        running_sum = jnp.sum(jnp.exp(scores - new_max[..., None]), axis=-1)
        return (new_max, running_sum)

    running_max, running_sum = over_keys(
        normalizer_piece,
        (
            jnp.full((heads_here, tok_rows), -1e30, jnp.float32),
            jnp.zeros((heads_here, tok_rows), jnp.float32),
        ),
    )
    log_total = running_max + jnp.log(running_sum)

    def value_piece(weighted, kv_piece, row_start):
        scores, key_heads, value_heads = piece_scores(kv_piece)
        weights = jnp.exp(scores - log_total[..., None])
        return jnp.einsum(
            "hqk,khd->qhd",
            weights.astype(jnp.bfloat16),
            value_heads,
            preferred_element_type=jnp.float32,
        )

    attended = over_keys(value_piece, jnp.zeros((tok_rows, heads_here, HD), jnp.float32))
    attended_low = attended.reshape(tok_rows, local_width).astype(jnp.bfloat16)
    back_rows = (
        jnp.zeros((peer_count * capacity, local_width), jnp.bfloat16)
        .at[from_slot]
        .set(attended_low)
    )
    returned = lax.all_to_all(
        back_rows.reshape(peer_count, capacity, local_width),
        "tok",
        split_axis=0,
        concat_axis=0,
        tiled=True,
    ).reshape(peer_count * capacity, local_width)[send_slot]
    attn_sum = lax.psum(
        jnp.dot(returned, out_weight, preferred_element_type=jnp.float32).astype(jnp.bfloat16),
        "head",
    ).astype(jnp.float32)
    middle = residual + attn_sum
    normed_two, inverse_two = layer_norm(middle)
    input_two = (normed_two * gain_two).astype(jnp.bfloat16)
    hidden = jnp.dot(input_two, up_weight, preferred_element_type=jnp.float32)
    active = jax.nn.gelu(hidden, approximate=True).astype(jnp.bfloat16)
    mlp_sum = lax.psum(
        jnp.dot(active, down_weight, preferred_element_type=jnp.float32).astype(jnp.bfloat16),
        "head",
    ).astype(jnp.float32)
    layer_out = (middle + mlp_sum).astype(jnp.bfloat16)
    grad_active = jnp.einsum(
        "td,fd->tf", cotangent, down_weight, preferred_element_type=jnp.float32
    )
    unused_value, gelu_pull = jax.vjp(
        lambda values_in: jax.nn.gelu(values_in, approximate=True), hidden
    )
    grad_hidden = gelu_pull(grad_active)[0].astype(jnp.bfloat16)
    grad_down = jnp.einsum("tf,td->fd", active, cotangent, preferred_element_type=jnp.float32)
    grad_up = jnp.einsum("td,tf->df", input_two, grad_hidden, preferred_element_type=jnp.float32)
    grad_in_two = lax.psum(
        jnp.einsum("tf,df->td", grad_hidden, up_weight, preferred_element_type=jnp.float32).astype(
            jnp.bfloat16
        ),
        "head",
    ).astype(jnp.float32)
    gain_two_grad = jnp.einsum("tm,td->md", onehot, grad_in_two * normed_two, precision=highest)
    grad_middle = cotangent.astype(jnp.float32) + norm_back(
        grad_in_two * gain_two, normed_two, inverse_two
    )
    grad_mid_low = grad_middle.astype(jnp.bfloat16)
    grad_out = jnp.einsum("tl,td->ld", returned, grad_mid_low, preferred_element_type=jnp.float32)
    grad_returned = jnp.einsum(
        "td,ld->tl", grad_mid_low, out_weight, preferred_element_type=jnp.float32
    ).astype(jnp.bfloat16)
    grad_rows = (
        jnp.zeros((peer_count * capacity, local_width), jnp.bfloat16)
        .at[send_slot]
        .set(grad_returned)
    )
    grad_heads = lax.all_to_all(
        grad_rows.reshape(peer_count, capacity, local_width),
        "tok",
        split_axis=0,
        concat_axis=0,
        tiled=True,
    ).reshape(peer_count * capacity, local_width)[from_slot]
    grad_heads = grad_heads.reshape(tok_rows, heads_here, HD)
    delta = jnp.sum(grad_heads.astype(jnp.float32) * attended, axis=-1).T
    kv_piece = lax.all_gather(keys_values, "tok", axis=0, tiled=True)
    key_count = kv_piece.shape[0]
    scores, key_heads, value_heads = piece_scores(kv_piece)
    weights = jnp.exp(scores - log_total[..., None])
    grad_weights = jnp.einsum(
        "qhd,khd->hqk", grad_heads, value_heads, preferred_element_type=jnp.float32
    )
    grad_scores = (weights * (grad_weights - delta[..., None])).astype(jnp.bfloat16)
    weights, grad_scores, key_heads = (weights, grad_scores, key_heads)
    grad_query = (
        jnp.einsum("hqk,khd->qhd", grad_scores, key_heads, preferred_element_type=jnp.float32)
        * score_scale
    )
    grad_keys = (
        jnp.einsum("hqk,qhd->khd", grad_scores, queries, preferred_element_type=jnp.float32)
        * score_scale
    )
    grad_values = jnp.einsum(
        "hqk,qhd->khd", weights.astype(jnp.bfloat16), grad_heads, preferred_element_type=jnp.float32
    )
    update = jnp.stack(
        [grad_keys.reshape(key_count, local_width), grad_values.reshape(key_count, local_width)],
        axis=1,
    )
    grad_pairs = update
    back_result = (grad_query, grad_pairs)
    grad_query, grad_pairs = back_result
    grad_kv = lax.psum_scatter(
        grad_pairs.astype(jnp.bfloat16), "tok", scatter_dimension=0, tiled=True
    )
    grad_packed = jnp.concatenate(
        [grad_query.reshape(tok_rows, 1, local_width).astype(jnp.bfloat16), grad_kv], axis=1
    )
    grad_back = (
        jnp.zeros((peer_count * capacity, 3, local_width), jnp.bfloat16)
        .at[from_slot]
        .set(grad_packed)
    )
    grad_arrived = lax.all_to_all(
        grad_back.reshape(peer_count, capacity, 3, local_width),
        "tok",
        split_axis=0,
        concat_axis=0,
        tiled=True,
    ).reshape(peer_count * capacity, 3, local_width)[send_slot]
    grad_query_a = rotate_back(
        grad_arrived[:, 0].astype(jnp.float32).reshape(tok_rows, heads_here, HD), cosine, sine
    )
    grad_key_a = rotate_back(
        grad_arrived[:, 1].astype(jnp.float32).reshape(tok_rows, heads_here, HD), cosine, sine
    )
    grad_proj = jnp.stack(
        [
            grad_query_a.reshape(tok_rows, local_width).astype(jnp.bfloat16),
            grad_key_a.reshape(tok_rows, local_width).astype(jnp.bfloat16),
            grad_arrived[:, 2],
        ],
        axis=1,
    )
    grad_in_one = lax.psum(
        jnp.einsum("tkh,dkh->td", grad_proj, qkv_weight, preferred_element_type=jnp.float32).astype(
            jnp.bfloat16
        ),
        "head",
    ).astype(jnp.float32)
    grad_qkv = jnp.einsum("td,tkh->dkh", input_one, grad_proj, preferred_element_type=jnp.float32)
    gain_one_grad = jnp.einsum("tm,td->md", onehot, grad_in_one * normed_one, precision=highest)
    grad_input = grad_middle + norm_back(grad_in_one * gain_one, normed_one, inverse_one)
    gains_grad = jnp.concatenate([gain_one_grad, gain_two_grad], axis=0)
    shares = (
        lax.psum_scatter(
            grad_qkv.astype(jnp.bfloat16), "tok", scatter_dimension=0, tiled=True
        ).astype(jnp.float32),
        lax.psum_scatter(
            grad_out.astype(jnp.bfloat16), "tok", scatter_dimension=0, tiled=True
        ).astype(jnp.float32),
        lax.psum_scatter(
            grad_up.astype(jnp.bfloat16), "tok", scatter_dimension=0, tiled=True
        ).astype(jnp.float32),
        lax.psum_scatter(
            grad_down.astype(jnp.bfloat16), "tok", scatter_dimension=0, tiled=True
        ).astype(jnp.float32),
        lax.psum_scatter(
            gains_grad.T.astype(jnp.bfloat16), "tok", scatter_dimension=0, tiled=True
        ).astype(jnp.float32),
    )
    return (layer_out, grad_input, shares[4].T, shares[0], shares[1], shares[2], shares[3])


def solution(mesh):
    return jax.shard_map(
        per_device,
        mesh=mesh,
        in_specs=(
            P("tok", None),
            P("tok"),
            P("tok"),
            P(),
            P(None, None, "head"),
            P("head", None),
            P(None, "head"),
            P("head", None),
            P("tok", None),
        ),
        out_specs=(
            P("tok", None),
            P("tok", None),
            P(None, "tok"),
            P("tok", None, "head"),
            P(("head", "tok"), None),
            P("tok", "head"),
            P(("head", "tok"), None),
        ),
        check_vma=False,
    )
```

profile of v0, /device:TPU:0, one launch (start us, length us, event | category | flops | bytes accessed | tf_op | source)
XLA Modules:
  0.0 1439.6 jit_solution(11969597995403496662)
XLA Ops:
  50.6 31.2 %scatter_fusion = bf16[512,3,512]{2,1,0:T(4,128)(2,1)} fusion(bf16[512,3,512]{2,1,0:T(4,128)(2,1)} %broadcast.353.clone, s32[256]{0:T(256)S(1)} %copy-done.46, bf16[256,3,512]{2,1,0:T(4,128)(2,1)} %copy.42), kind=kCustom, calls=%fused_computation.6 | custom fusion | bytes 2360320 | tf_op jit(solution)/shard_map/scatter | solution.py:118
  131.8 65.1 %all-gather.2.cloned.1.call-done = bf16[8192,2,512]{2,1,0:T(2,128)(2,1)} async-done(((bf16[256,2,512]{2,1,0:T(2,128)(2,1)}), bf16[8192,2,512]{2,1,0:T(2,128)(2,1)}) %all-gather.2.cloned.1.call-update) | async-done | bytes 16777232 | tf_op jit(solution)/shard_map/all_gather | solution.py:156
  196.9 33.0 %fusion.69 = (bf16[8192,1,512]{2,1,0:T(2,128)(2,1)}, bf16[8192,1,512]{2,1,0:T(2,128)(2,1)}) fusion(bf16[8192,2,512]{2,1,0:T(2,128)(2,1)} %all-gather.2.cloned.1.call-done), kind=kLoop, calls=%fused_computation.178 | loop fusion | bytes 33554432 | tf_op jit(solution)/shard_map/slice | solution.py:145
  229.8 33.4 %copy.71 = bf16[8192,1,512]{0,2,1:T(8,128)(2,1)} copy(bf16[8192,1,512]{2,1,0:T(2,128)(2,1)} %get-tuple-element.16) | data formatting | bytes 16777216
  263.2 18.5 %fusion.1 = (f32[4,256]{1,0:T(4,128)S(1)}, f32[4,256,8192]{2,1,0:T(8,128)}) fusion(pred[256,8192]{1,0:T(8,128)(4,1)} %compare_and_fusion, bf16[256,4,128]{0,2,1:T(8,128)(2,1)S(1)} %bitcast.110, bf16[8192,4,128]{0,2,1:T(8,128)(2,1)} %bitcast.97), kind=kOutput, calls=%fused_computation.15 | convolution fusion | flops 2172648448 | bytes 44306432 | tf_op jit(solution)/shard_map/qhd,khd->hqk/dot_general | solution.py:148
  281.7 15.2 %exponential_reduce_fusion = f32[4,256]{1,0:T(4,128)S(1)} fusion(f32[4,256,8192]{2,1,0:T(8,128)} %get-tuple-element.44, f32[4,256]{1,0:T(4,128)S(1)} %broadcast_maximum_fusion, pred[256,8192]{1,0:T(8,128)(4,1)} %compare_and_fusion), kind=kLoop, calls=%fused_computation.12 | loop fusion | flops 33553408 | bytes 35659776 | tf_op jit(solution)/shard_map/reduce_sum | solution.py:164
  296.9 33.4 %copy.45 = bf16[8192,1,512]{0,2,1:T(8,128)(2,1)} copy(bf16[8192,1,512]{2,1,0:T(2,128)(2,1)} %get-tuple-element.17) | data formatting | bytes 16777216 | tf_op jit(solution)/shard_map/slice | solution.py:146
  330.3 17.5 %fusion.74 = (bf16[256,4,128]{0,2,1:T(8,128)(2,1)S(1)}, f32[256,4,128]{0,2,1:T(8,128)}) fusion(bf16[8192,4,128]{0,2,1:T(8,128)(2,1)} %bitcast.103, f32[4,256,8192]{2,1,0:T(8,128)} %get-tuple-element.44, f32[4,256]{1,0:T(4,128)S(1)} %log_add_fusion, pred[256,8192]{1,0:T(8,128)(4,1)} %compare_and_fusion), kind=kOutput, calls=%fused_computation.183 | convolution fusion | flops 2181169152 | bytes 44830720 | tf_op jit(solution)/shard_map/hqk,khd->qhd/dot_general | solution.py:179
  380.0 36.5 %all-reduce.7.cloned.1.call-done = bf16[256,2048]{1,0:T(8,128)(2,1)} async-done(((bf16[256,2048]{1,0:T(8,128)(2,1)}), bf16[256,2048]{1,0:T(8,128)(2,1)}) %all-reduce.7.cloned.1.call-update) | async-done | bytes 1048592 | tf_op jit(solution)/shard_map/psum | solution.py:200
  434.7 46.6 %all-reduce.9.cloned.1.call-done = bf16[256,2048]{1,0:T(8,128)(2,1)} async-done(((bf16[256,2048]{1,0:T(8,128)(2,1)}), bf16[256,2048]{1,0:T(8,128)(2,1)}) %all-reduce.9.cloned.1.call-update) | async-done | bytes 1048592 | tf_op jit(solution)/shard_map/psum | solution.py:223
  491.0 18.3 %all_to_all.29 = bf16[32,16,512]{2,1,0:T(8,128)(2,1)S(1)} all-to-all(bf16[32,16,512]{2,1,0:T(8,128)(2,1)S(1)} %bitcast.109), channel_id=1, replica_groups=mesh['tok'=32,'head'=4] {'tok'}, dimensions={0} | all-to-all | bytes 1048576 | tf_op jit(solution)/shard_map/all_to_all | solution.py:243
  511.3 19.1 %convolution_convert_fusion = bf16[4,128,8192]{2,1,0:T(8,128)(2,1)} fusion(bf16[256,4,128]{0,2,1:T(8,128)(2,1)} %bitcast.113, f32[4,256,8192]{2,1,0:T(8,128)} %get-tuple-element.44, f32[4,256]{1,0:T(4,128)S(1)} %log_add_fusion, pred[256,8192]{1,0:T(8,128)(4,1)} %compare_and_fusion), kind=kOutput, calls=%fused_computation.18 | convolution fusion | flops 2185232384 | bytes 44306432 | tf_op jit(solution)/shard_map/hqk,qhd->khd/dot_general | solution.py:269
  530.4 24.7 %multiply_convert_fusion = bf16[4,256,8192]{2,1,0:T(8,128)(2,1)} fusion(f32[4,256,8192]{2,1,0:T(8,128)} %get-tuple-element.44, bf16[256,4,128]{0,2,1:T(8,128)(2,1)} %bitcast.114, bf16[8192,4,128]{0,2,1:T(8,128)(2,1)} %bitcast.104, f32[4,256]{1,0:T(4,128)S(1)} %bitcast.117, f32[4,256]{1,0:T(4,128)S(1)} %log_add_fusion, pred[256,8192]{1,0:T(8,128)(4,1)S(1)} %copy-done.13), kind=kOutput, calls=%fused_computation.10 | convolution fusion | flops 2197815296 | bytes 61087744 | tf_op jit(solution)/shard_map/qhd,khd->hqk/dot_general | solution.py:256
  567.3 34.7 %copy.54 = bf16[8192,1,512]{2,1,0:T(2,128)(2,1)} copy(bf16[8192,1,512]{0,2,1:T(8,128)(2,1)} %bitcast.99) | data formatting | bytes 16777216 | tf_op jit(solution)/shard_map/stack;reshape | solution.py:272
  602.0 34.6 %copy.55 = bf16[8192,1,512]{2,1,0:T(2,128)(2,1)} copy(bf16[8192,1,512]{0,2,1:T(8,128)(2,1)} %bitcast.105) | data formatting | bytes 16777216 | tf_op jit(solution)/shard_map/stack;reshape | solution.py:272
  636.6 37.7 %pad_maximum_fusion = bf16[8192,2,512]{2,1,0:T(2,128)(2,1)} fusion(bf16[8192,1,512]{2,1,0:T(2,128)(2,1)} %copy.55, bf16[8192,1,512]{2,1,0:T(2,128)(2,1)} %copy.54), kind=kLoop, calls=%fused_computation.16 | loop fusion | flops 33554432 | bytes 33554432 | tf_op jit(solution)/shard_map/stack | solution.py:272
  688.7 163.3 %all-reduce.11.cloned.1.call-done = bf16[8192,2,512]{2,1,0:T(2,128)(2,1)} async-done(((bf16[8192,2,512]{2,1,0:T(2,128)(2,1)}), bf16[8192,2,512]{2,1,0:T(2,128)(2,1)}) %all-reduce.11.cloned.1.call-update) | async-done | bytes 16777232
  855.9 20.1 %scatter_fusion.1 = bf16[512,3,512]{2,1,0:T(4,128)(2,1)S(1)} fusion(bf16[512,3,512]{2,1,0:T(4,128)(2,1)S(1)} %broadcast.353, s32[256]{0:T(256)S(1)} %compare_select_fusion.2, bf16[256,3,512]{2,1,0:T(4,128)(2,1)} %pad_maximum_fusion.1), kind=kCustom, calls=%fused_computation.9 | custom fusion | bytes 2360320 | tf_op jit(solution)/shard_map/scatter | solution.py:288
  953.0 33.9 %all-reduce.13.cloned.1.call-done = (bf16[256,2048]{1,0:T(8,128)(2,1)}, bf16[256,2048]{1,0:T(8,128)(2,1)}) async-done(((bf16[256,2048]{1,0:T(8,128)(2,1)}, bf16[256,2048]{1,0:T(8,128)(2,1)}), (bf16[256,2048]{1,0:T(8,128)(2,1)}, bf16[256,2048]{1,0:T(8,128)(2,1)})) %all-reduce.13.cloned.1.call-update) | async-done | bytes 2097168 | tf_op jit(solution)/shard_map/psum | solution.py:209
  995.1 74.6 %reduce-scatter.10.cloned.1.call-done = bf16[16,2048]{1,0:T(8,128)(2,1)} async-done(((bf16[512,2048]{1,0:T(8,128)(2,1)}), bf16[16,2048]{1,0:T(8,128)(2,1)}) %reduce-scatter.10.cloned.1.call-update) | async-done | bytes 65552 | tf_op jit(solution)/shard_map/reduce_scatter | solution.py:325
  1071.2 94.3 %reduce-scatter.12.cloned.1.call-done = bf16[64,2048]{1,0:T(8,128)(2,1)} async-done(((bf16[2048,2048]{1,0:T(8,128)(2,1)}), bf16[64,2048]{1,0:T(8,128)(2,1)}) %reduce-scatter.12.cloned.1.call-update) | async-done | bytes 262160 | tf_op jit(solution)/shard_map/reduce_scatter | solution.py:328
  1167.3 94.4 %reduce-scatter.14.cloned.1.call-done = bf16[64,2048]{1,0:T(8,128)(2,1)} async-done(((bf16[2048,2048]{1,0:T(8,128)(2,1)}), bf16[64,2048]{1,0:T(8,128)(2,1)}) %reduce-scatter.14.cloned.1.call-update) | async-done | bytes 262160 | tf_op jit(solution)/shard_map/reduce_scatter | solution.py:331
  1270.7 70.9 %reduce-scatter.16.cloned.1.call-done = bf16[64,6]{1,0:T(8,128)(2,1)} async-done(((bf16[2048,6]{1,0:T(8,128)(2,1)}), bf16[64,6]{1,0:T(8,128)(2,1)}) %reduce-scatter.16.cloned.1.call-update) | async-done | bytes 784
  1343.0 87.8 %reduce-scatter.8.cloned.1.call-done = bf16[64,3,512]{2,0,1:T(8,128)(2,1)} async-done(((bf16[2048,3,512]{2,0,1:T(8,128)(2,1)}), bf16[64,3,512]{2,0,1:T(8,128)(2,1)}) %reduce-scatter.8.cloned.1.call-update) | async-done | bytes 196624 | tf_op jit(solution)/shard_map/reduce_scatter | solution.py:322
  (258 shorter events, 285.0 us)
Async XLA Ops:
  7.2 363.6 %copy-start = (bf16[512,2048]{1,0:T(8,128)(2,1)S(1)}, bf16[512,2048]{1,0:T(8,128)(2,1)}, u32[]{:S(2)}) copy-start(bf16[512,2048]{1,0:T(8,128)(2,1)} %param.14) | copy-start | bytes 6291460
  11.1 73.9 %all-to-all-start = ((s32[32,1,16]{2,1,0:T(1,128)}), s32[32,1,16]{2,1,0:T(1,128)S(1)}, u32[]{:S(2)}, u32[]{:S(2)}) async-start(s32[32,1,16]{2,1,0:T(1,128)} %bitcast.2), calls=%async_computation | async-start | bytes 32768 | tf_op jit(solution)/shard_map/all_to_all | solution.py:109
  85.0 30.6 %all-to-all-start.1 = ((bf16[32,16,3,512]{3,1,2,0:T(8,128)(2,1)}), bf16[32,16,3,512]{3,1,2,0:T(8,128)(2,1)}, u32[]{:S(2)}, u32[]{:S(2)}) async-start(bf16[32,16,3,512]{3,1,2,0:T(8,128)(2,1)} %copy.43), calls=%async_computation.1 | async-start | bytes 3145728 | tf_op jit(solution)/shard_map/all_to_all | solution.py:120
  92.5 104.3 %all-gather.2.cloned.1.call-start = ((), (), s32[]{:S(2)}) async-start(), calls=%async_computation.10 | async-start | bytes 17301504 | tf_op jit(solution)/shard_map/all_gather | solution.py:156
  131.8 131.4 %copy-start.24 = (bf16[256,1,512]{0,2,1:T(8,128)(2,1)}, bf16[256,1,512]{0,2,1:T(8,128)(2,1)S(1)}, u32[]{:S(2)}) copy-start(bf16[256,1,512]{0,2,1:T(8,128)(2,1)S(1)} %copy.46) | copy-start | bytes 786436
  351.8 16.7 %all-to-all-start.2 = ((bf16[32,16,512]{2,1,0:T(8,128)(2,1)}), bf16[32,16,512]{2,1,0:T(8,128)(2,1)}, u32[]{:S(2)}, u32[]{:S(2)}) async-start(bf16[32,16,512]{2,1,0:T(8,128)(2,1)} %bitcast.108), calls=%async_computation.2 | async-start | bytes 1048576 | tf_op jit(solution)/shard_map/all_to_all | solution.py:193
  357.3 59.2 %all-reduce.7.cloned.1.call-start = ((), (), s32[]{:S(2)}) async-start(), calls=%async_computation.11 | async-start | bytes 2097152 | tf_op jit(solution)/shard_map/psum | solution.py:200
  372.5 108.8 %all-reduce.9.cloned.1.call-start = ((), (), s32[]{:S(2)}) async-start(), calls=%async_computation.12 | async-start | bytes 2097152 | tf_op jit(solution)/shard_map/psum | solution.py:223
  380.0 38.8 %copy-start.34 = (f32[6,2048]{1,0:T(8,128)S(1)}, f32[6,2048]{1,0:T(8,128)}, u32[]{:S(2)}) copy-start(f32[6,2048]{1,0:T(8,128)} %param.12) | copy-start | bytes 147460
  380.0 38.8 %copy-start.48 = (s32[256]{0:T(256)S(1)}, s32[256]{0:T(256)}, u32[]{:S(2)}) copy-start(s32[256]{0:T(256)} %param.10) | copy-start | bytes 3076
  434.5 417.4 %all-reduce.11.cloned.1.call-start = ((), (), s32[]{:S(2)}) async-start(), calls=%async_computation.18 | async-start | bytes 33554432
  877.7 28.9 %all-to-all-start.4 = ((bf16[32,16,3,512]{3,1,2,0:T(8,128)(2,1)}), bf16[32,16,3,512]{3,1,2,0:T(8,128)(2,1)S(1)}, u32[]{:S(2)}, u32[]{:S(2)}) async-start(bf16[32,16,3,512]{3,1,2,0:T(8,128)(2,1)} %copy.57), calls=%async_computation.4 | async-start | bytes 3145728 | tf_op jit(solution)/shard_map/all_to_all | solution.py:290
  883.4 103.6 %all-reduce.13.cloned.1.call-start = ((), (), s32[]{:S(2)}) async-start(), calls=%async_computation.19 | async-start | bytes 4194304 | tf_op jit(solution)/shard_map/psum | solution.py:209
  930.5 139.2 %reduce-scatter.10.cloned.1.call-start = ((), (), s32[]{:S(2)}) async-start(), calls=%async_computation.14 | async-start | bytes 2162688 | tf_op jit(solution)/shard_map/reduce_scatter | solution.py:325
  934.2 231.3 %reduce-scatter.12.cloned.1.call-start = ((), (), s32[]{:S(2)}) async-start(), calls=%async_computation.15 | async-start | bytes 8650752 | tf_op jit(solution)/shard_map/reduce_scatter | solution.py:328
  941.4 320.4 %reduce-scatter.14.cloned.1.call-start = ((), (), s32[]{:S(2)}) async-start(), calls=%async_computation.16 | async-start | bytes 8650752 | tf_op jit(solution)/shard_map/reduce_scatter | solution.py:331
  950.2 391.4 %reduce-scatter.16.cloned.1.call-start = ((), (), s32[]{:S(2)}) async-start(), calls=%async_computation.17 | async-start | bytes 540672
  953.0 37.6 %copy-start.29 = (bf16[256,2048,1]{1,0,2:T(8,128)(2,1)S(1)}, bf16[256,2048,1]{1,0,2:T(8,128)(2,1)}, u32[]{:S(2)}) copy-start(bf16[256,2048,1]{1,0,2:T(8,128)(2,1)} %copy-done.28) | copy-start | bytes 3145732
  953.0 37.6 %copy-start.36 = (bf16[256,1,512]{2,0,1:T(8,128)(2,1)S(1)}, bf16[256,1,512]{2,0,1:T(8,128)(2,1)}, u32[]{:S(2)}) copy-start(bf16[256,1,512]{2,0,1:T(8,128)(2,1)} %copy-done.35) | copy-start | bytes 786436
  953.0 37.6 %copy-start.38 = (bf16[256,1,512]{2,0,1:T(8,128)(2,1)S(1)}, bf16[256,1,512]{2,0,1:T(8,128)(2,1)}, u32[]{:S(2)}) copy-start(bf16[256,1,512]{2,0,1:T(8,128)(2,1)} %copy-done.37) | copy-start | bytes 786436
  953.0 37.6 %copy-start.40 = (bf16[256,1,512]{2,0,1:T(8,128)(2,1)S(1)}, bf16[256,1,512]{2,0,1:T(8,128)(2,1)}, u32[]{:S(2)}) copy-start(bf16[256,1,512]{2,0,1:T(8,128)(2,1)} %copy-done.39) | copy-start | bytes 786436
  990.5 440.3 %reduce-scatter.8.cloned.1.call-start = ((), (), s32[]{:S(2)}) async-start(), calls=%async_computation.13 | async-start | bytes 6488064 | tf_op jit(solution)/shard_map/reduce_scatter | solution.py:322
  995.1 268.4 %copy-start.8 = (f32[256,2048]{1,0:T(8,128)S(1)}, f32[256,2048]{1,0:T(8,128)}, u32[]{:S(2)}) copy-start(f32[256,2048]{1,0:T(8,128)} %copy-done.7) | copy-start | bytes 6291460
  1266.0 166.6 %copy-start.1 = (bf16[512,2048]{1,0:T(8,128)(2,1)S(1)}, bf16[512,2048]{1,0:T(8,128)(2,1)}, u32[]{:S(2)}) copy-start(bf16[512,2048]{1,0:T(8,128)(2,1)} %param.14) | copy-start | bytes 6291460
  (44 other events, 255.0 us)
Sparse Core Ops, SparseCore 0:
  126.6 70.2 all-gather.1
  372.6 43.8 all-reduce.6
  434.6 46.6 all-reduce.8
  674.4 177.4 all-reduce.10
  930.6 56.3 all-reduce.12
  991.0 78.7 reduce-scatter.9
  1073.4 92.0 reduce-scatter.11
  1169.7 92.0 reduce-scatter.13
  1265.2 76.3 reduce-scatter.15
  1345.2 85.6 reduce-scatter.7
where the time goes:
time: 1450 us; the launch traced here: 1440 us
  waiting for transfers between devices  802 us (55%)
  local copies, waits for them, and re-layouts  300 us (21%)
  matrix products  169 us (12%)
  other arithmetic  95.4 us (7%)
  starting transfers between devices  39.7 us (3%)
  blocking collectives  18.3 us (1%)
  between operations  15.8 us (1%)
    unnamed x12, waiting for transfers between devices  234 us
    reduce_scatter x1, waiting for transfers between devices, per_device(): lax.psum_scatter(grad_down.astype(jnp.bfloat16), 'tok', scatter_dimension...  94.4 us
    reduce_scatter x1, waiting for transfers between devices, per_device(): lax.psum_scatter(grad_up.astype(jnp.bfloat16), 'tok', scatter_dimension=0...  94.3 us
    reduce_scatter x1, waiting for transfers between devices, per_device(): lax.psum_scatter(grad_qkv.astype(jnp.bfloat16), 'tok', scatter_dimension=...  87.8 us
    reduce_scatter x1, waiting for transfers between devices, per_device(): lax.psum_scatter(grad_out.astype(jnp.bfloat16), 'tok', scatter_dimension=...  74.6 us
    another operation x2, local copies, waits for them, and re-layouts, per_device(): jnp.stack([grad_keys.reshape(key_count, local_width), grad_values.reshape...  69.3 us
    all_gather x1, waiting for transfers between devices, over_keys(): lax.all_gather(keys_values, 'tok', axis=0, tiled=True)  65.1 us
    unnamed x114, local copies, waits for them, and re-layouts  51.7 us
  transfers between devices with their start and end apart: 14, of which 13 were waited for; matrix products, arithmetic and copies ran while one was open for 10% of the time, Pallas kernels for 0%

commit v1 on v0

v1 whole, which is shorter than its diff:
```python
import functools
import math

import jax
import jax.numpy as jnp
from jax import lax
from jax.experimental import pallas as pl
from jax.experimental.pallas import tpu as pltpu
from jax.sharding import PartitionSpec as P

HD = 128
SIDE = 4
ROWS = 256
CLIP_STEP = 8192
MESH = pl.DeviceIdType.MESH
NT = (((1,), (1,)), ((), ()))
TN = (((0,), (0,)), ((), ()))
NN = (((1,), (0,)), ((), ()))
f32 = jnp.float32
bf16 = jnp.bfloat16
highest = lax.Precision.HIGHEST
VMEM_LIMIT = 56 << 20
HOPS = (1, 3, 2)


def dot(lhs, rhs, dims=NN):
    return lax.dot_general(lhs, rhs, dims, preferred_element_type=f32)


def place():
    tok = lax.axis_index("tok")
    return (lax.div(tok, 8), lax.axis_index("head"), lax.rem(lax.div(tok, 2), 4), lax.rem(tok, 2))


def around(index, step):
    return lax.rem(index + (step % SIDE), SIDE)


def device(x, y, z, core):
    return (x * 8 + z * 2 + core, y)


def remote(src, dst, send_sem, recv_sem, target):
    return pltpu.make_async_remote_copy(
        src_ref=src,
        dst_ref=dst,
        send_sem=send_sem,
        recv_sem=recv_sem,
        device_id=target,
        device_id_type=MESH,
    )


def meet(targets):
    barrier = pltpu.get_barrier_semaphore()
    for target in targets:
        pl.semaphore_signal(barrier, inc=1, device_id=target, device_id_type=MESH)
    pl.semaphore_wait(barrier, len(targets))


class Copies:
    def __init__(self, send_sems, recv_sems):
        self.send_sems = send_sems
        self.recv_sems = recv_sems
        self.used = 0
        self.open = []

    def start(self, src, dst, target, landing):
        index = self.used
        self.used += 1
        copy = remote(src, dst, self.send_sems.at[index], self.recv_sems.at[index], target)
        copy.start()
        self.open.append(copy)
        return remote(landing, landing, self.send_sems.at[index], self.recv_sems.at[index], target)

    def finish(self):
        for copy in self.open:
            copy.wait_send()


def sum_over_y(copies, here, given, came, total):
    x, y, z, core = here
    arrivals = []
    for n, hop in enumerate(HOPS):
        other = around(y, hop)
        arrivals.append(
            copies.start(given.at[other], came.at[n], device(x, other, z, core), came.at[n])
        )
    yield
    for arrival in arrivals:
        arrival.wait_recv()
    total[y] = (
        (given[y].astype(f32) + came[0].astype(f32))
        + (came[1].astype(f32) + came[2].astype(f32))
    ).astype(bf16)
    arrivals = []
    for hop in HOPS:
        arrivals.append(
            copies.start(
                total.at[y],
                total.at[y],
                device(x, around(y, hop), z, core),
                total.at[around(y, -hop)],
            )
        )
    yield
    for arrival in arrivals:
        arrival.wait_recv()
    yield


def ring_sum(copies, own, towards, block, slots):
    up, down = towards(1), towards(-1)
    from_down = copies.start(block(2, 0), slots.at[0], up, slots.at[0])
    from_up = copies.start(block(2, 1), slots.at[1], down, slots.at[1])
    raw_down = copies.start(block(1, 1), slots.at[2], up, slots.at[2])
    raw_up = copies.start(block(-1, 0), slots.at[3], down, slots.at[3])
    yield
    from_down.wait_recv()
    onward = block(1, 0)
    onward[...] = (onward[...].astype(f32) + slots[0].astype(f32)).astype(bf16)
    sum_down = copies.start(onward, slots.at[4], up, slots.at[4])
    from_up.wait_recv()
    onward = block(-1, 1)
    onward[...] = (onward[...].astype(f32) + slots[1].astype(f32)).astype(bf16)
    sum_up = copies.start(onward, slots.at[5], down, slots.at[5])
    yield
    for arrival in (raw_down, raw_up, sum_down, sum_up):
        arrival.wait_recv()

    def finished(half):
        mine = block(0, half)[...].astype(f32)
        if half == 0:
            return mine + slots[4].astype(f32) + slots[3].astype(f32)
        return mine + slots[2].astype(f32) + slots[5].astype(f32)

    own.append(finished)


def weight_scratch(rows, cols):
    half = cols // 4
    return [
        pltpu.VMEM((16, rows, 2 * ROWS), bf16),
        pltpu.VMEM((2 * ROWS, cols), bf16),
        pltpu.VMEM((2, 4, 2, 4 * rows, half), bf16),
        pltpu.VMEM((2, 6, 4 * rows, half), bf16),
        pltpu.VMEM((2, 2, 4, rows, half), bf16),
        pltpu.VMEM((2, 6, rows, half), bf16),
        pltpu.SemaphoreType.DMA((26,)),
        pltpu.SemaphoreType.DMA((26,)),
        pltpu.SemaphoreType.DMA((2,)),
    ]


def weight_grad(here, left, right, out, scratch):
    both_left, both_right, parts, came, sums, late, send_sems, recv_sems, own_sems = scratch
    x, y, z, core = here
    rows, cols = out.shape
    half = cols // 4
    copies = Copies(send_sems, recv_sems)
    twin = device(x, y, z, 1 - core)
    own_left = pltpu.make_async_copy(
        left.at[:, core], both_left.at[:, :, pl.ds(0, ROWS)], own_sems.at[0]
    )
    own_right = pltpu.make_async_copy(right, both_right.at[pl.ds(0, ROWS)], own_sems.at[1])
    own_left.start()
    own_right.start()
    far_left = copies.start(
        left.at[:, 1 - core],
        both_left.at[:, :, pl.ds(ROWS, ROWS)],
        twin,
        both_left.at[:, :, pl.ds(ROWS, ROWS)],
    )
    far_right = copies.start(
        right,
        both_right.at[pl.ds(ROWS, ROWS)],
        twin,
        both_right.at[pl.ds(ROWS, ROWS)],
    )
    yield
    own_left.wait()
    own_right.wait()
    far_left.wait_recv()
    far_right.wait_recv()

    def spot(way, step):
        return around(x if way == 0 else z, step)

    def fill(way, step, half_index):
        at = spot(way, step)
        if way == 0:
            chosen = both_left[pl.ds(at * 4, 4)].reshape(4 * rows, 2 * ROWS)
        else:
            chosen = jnp.concatenate([both_left[k * 4 + at] for k in range(4)], axis=0)
        start = (way * 2 + half_index) * half
        parts[way, at, half_index] = dot(chosen, both_right[:, start : start + half]).astype(bf16)

    def towards(way):
        def target(step):
            if way == 0:
                return device(around(x, step), y, z, core)
            return device(x, y, around(z, step), core)

        return target

    first, first_done = [], ([], [])
    for way in (0, 1):
        for step, half_index in ((2, 0), (2, 1), (1, 1), (-1, 0)):
            fill(way, step, half_index)
        ring = ring_sum(
            copies,
            first_done[way],
            towards(way),
            lambda step, half_index, way=way: parts.at[way, spot(way, step), half_index],
            came.at[way],
        )
        next(ring)
        first.append(ring)
    for way in (0, 1):
        for step, half_index in ((1, 0), (-1, 1), (0, 0), (0, 1)):
            fill(way, step, half_index)
    yield
    for ring in first:
        next(ring)
    yield
    second, second_done = [], ([], [])
    for way in (0, 1):
        next(first[way], None)
        for half_index in (0, 1):
            sums[way, half_index] = (
                first_done[way][0](half_index).astype(bf16).reshape(4, rows, half)
            )
        ring = ring_sum(
            copies,
            second_done[way],
            towards(1 - way),
            lambda step, half_index, way=way: sums.at[way, half_index, spot(1 - way, step)],
            late.at[way],
        )
        next(ring)
        second.append(ring)
    yield
    for ring in second:
        next(ring)
    yield
    for way in (0, 1):
        next(second[way], None)
        for half_index in (0, 1):
            start = (way * 2 + half_index) * half
            out[:, start : start + half] = second_done[way][0](half_index)
    copies.finish()
    yield


def sum_kernel(shapes, *refs):
    count = len(shapes)
    given = refs[0]
    factors = refs[1 : 1 + 2 * count]
    total = refs[1 + 2 * count]
    outs = refs[2 + 2 * count : 2 + 3 * count]
    came, all_rows, y_send, y_recv = refs[2 + 3 * count : 6 + 3 * count]
    scratch = refs[6 + 3 * count :]
    here = place()
    x, y, z, core = here
    meet(
        [device(x, around(y, hop), z, core) for hop in HOPS]
        + [device(around(x, hop), y, z, core) for hop in (1, 3)]
        + [device(x, y, around(z, hop), core) for hop in (1, 3)]
        + [device(x, y, z, 1 - core)]
    )
    copies = Copies(y_send, y_recv)
    over_y = sum_over_y(copies, here, given, came, all_rows)
    grads = [
        weight_grad(here, factors[2 * n], factors[2 * n + 1], outs[n], scratch[9 * n : 9 * n + 9])
        for n in range(count)
    ]
    next(over_y)
    for grad in grads:
        next(grad)
    for grad in grads:
        next(grad)
    next(over_y)
    for grad in grads:
        next(grad)
    next(over_y)
    total[...] = all_rows[...]
    copies.finish()
    for step in range(3):
        for grad in grads:
            next(grad)


def sum_and_grads(given, factors, collective_id):
    shapes = [(left.shape[2], right.shape[1]) for left, right in factors]
    width = given.shape[1]
    quarter = ROWS // SIDE
    flat = [array for pair in factors for array in pair]
    whole = pl.BlockSpec(memory_space=pltpu.VMEM)
    outs = pl.pallas_call(
        functools.partial(sum_kernel, shapes),
        out_shape=[jax.ShapeDtypeStruct((SIDE, quarter, width), bf16)]
        + [jax.ShapeDtypeStruct(shape, f32) for shape in shapes],
        in_specs=[whole] + [pl.BlockSpec(memory_space=pl.ANY)] * len(flat),
        out_specs=[whole] * (1 + len(shapes)),
        scratch_shapes=[
            pltpu.VMEM((3, quarter, width), bf16),
            pltpu.VMEM((SIDE, quarter, width), bf16),
            pltpu.SemaphoreType.DMA((6,)),
            pltpu.SemaphoreType.DMA((6,)),
        ]
        + [entry for shape in shapes for entry in weight_scratch(*shape)],
        compiler_params=pltpu.CompilerParams(
            collective_id=collective_id, has_side_effects=True, vmem_limit_bytes=VMEM_LIMIT
        ),
        name=f"sum_and_grads_{collective_id}",
    )(given.reshape(SIDE, quarter, width), *flat)
    return [outs[0].reshape(ROWS, width)] + list(outs[1:])


def visible(key_codes, low, span):
    return (key_codes - low).astype(jnp.uint32) <= span.astype(jnp.uint32)


def key_column(codes):
    row = lax.broadcasted_iota(jnp.int32, (8, HD), 0)
    weight = jnp.where(row == 0, 128.0, jnp.where(row == 1, 1.0, 0.0)).astype(bf16)
    return dot(codes, weight, TN).astype(jnp.int32)


QUERY_TILE = 512


def forward_kernel(
    q_ref, kv_ref, codes_ref, bounds_ref, out_weight_ref,
    q_all_ref, kv_all_ref, o_ref, lse_ref, returned_ref, total_ref,
    queries, keys_values, top, norm, acc, column, o_low, back, given, came, all_rows,
    send_sems, recv_sems, y_send, y_recv, keep_sems,
):
    here = place()
    x, y, z, core = here
    twin = device(x, y, z, 1 - core)
    meet(
        [device(around(x, hop), y, z, core) for hop in HOPS]
        + [device(x, around(y, hop), z, core) for hop in HOPS]
        + [device(x, y, around(z, hop), core) for hop in (1, 3)]
        + [twin]
    )
    copies = Copies(send_sems, recv_sems)
    above, below = device(x, y, around(z, 1), core), device(x, y, around(z, -1), core)
    next_z, last_z, far_z = around(z, 1), around(z, -1), around(z, 2)
    kv_came, q_came = [], []
    for hop in HOPS:
        other = around(x, hop)
        target = device(other, y, z, core)
        kv_came.append(
            copies.start(
                kv_ref.at[other],
                keys_values.at[z, core, x],
                target,
                keys_values.at[z, core, around(x, -hop)],
            )
        )
    for hop in HOPS:
        other = around(x, hop)
        target = device(other, y, z, core)
        q_came.append(
            copies.start(q_ref.at[other], queries.at[x], target, queries.at[around(x, -hop)])
        )
    keys_values[z, core, x] = kv_ref[x]
    queries[x] = q_ref[x]
    top[...] = jnp.full_like(top, -1e30)
    norm[...] = jnp.zeros_like(norm)
    acc[...] = jnp.zeros_like(acc)
    pieces = [x] + [around(x, -hop) for hop in HOPS]
    from_last, from_next, from_twin = [], [], []
    for n, piece in enumerate(pieces):
        if n > 0:
            kv_came[n - 1].wait_recv()
        block = keys_values.at[z, core, piece]
        from_last.append(copies.start(block, block, above, keys_values.at[last_z, core, piece]))
        from_next.append(copies.start(block, block, below, keys_values.at[next_z, core, piece]))
        from_twin.append(copies.start(block, block, twin, keys_values.at[z, 1 - core, piece]))
    for arrival in q_came:
        arrival.wait_recv()

    def attend(z_at, core_at):
        column[...] = key_column(codes_ref[z_at, core_at])

        def tile(index, carry):
            at = pl.ds(pl.multiple_of(index * QUERY_TILE, QUERY_TILE), QUERY_TILE)
            query = queries[pl.ds(index * 2, 2)].reshape(QUERY_TILE, HD)
            keys = keys_values[z_at, core_at, :, :, :HD].reshape(4 * ROWS, HD)
            values = keys_values[z_at, core_at, :, :, HD:].reshape(4 * ROWS, HD)
            scores = dot(keys, query, NT)
            codes = jnp.concatenate([column[...]] * (QUERY_TILE // HD), axis=1)
            seen = visible(codes, bounds_ref[0:1, at], bounds_ref[1:2, at])
            scores = jnp.where(seen, scores, -1e30)
            top_before = top[0:1, at]
            top_now = jnp.maximum(top_before, jnp.max(scores, axis=0, keepdims=True))
            weights = jnp.exp2(scores - top_now)
            shrink = jnp.exp2(top_before - top_now)
            norm[0:1, at] = norm[0:1, at] * shrink + jnp.sum(weights, axis=0, keepdims=True)
            top[0:1, at] = top_now
            acc[:, at] = acc[:, at] * shrink + dot(values, weights.astype(bf16), TN)
            return carry

        lax.fori_loop(0, 4 * ROWS // QUERY_TILE, tile, 0)

    low_far, high_far, twin_last, twin_next = [], [], [], []

    def onward(n):
        piece = pieces[n]
        from_last[n].wait_recv()
        block = keys_values.at[last_z, core, piece]
        low = block.at[pl.ds(0, ROWS // 2)]
        low_far.append(
            copies.start(low, low, above, keys_values.at[far_z, core, piece, pl.ds(0, ROWS // 2)])
        )
        twin_last.append(
            copies.start(block, block, twin, keys_values.at[last_z, 1 - core, piece])
        )
        from_next[n].wait_recv()
        block = keys_values.at[next_z, core, piece]
        high = block.at[pl.ds(ROWS // 2, ROWS // 2)]
        high_far.append(
            copies.start(
                high,
                high,
                below,
                keys_values.at[far_z, core, piece, pl.ds(ROWS // 2, ROWS // 2)],
            )
        )
        twin_next.append(
            copies.start(block, block, twin, keys_values.at[next_z, 1 - core, piece])
        )

    def take(arrivals):
        for arrival in arrivals:
            arrival.wait_recv()

    attend(z, core)
    onward(0)
    onward(1)
    take(from_twin)
    attend(z, 1 - core)
    onward(2)
    onward(3)
    attend(last_z, core)
    attend(next_z, core)
    take(twin_last)
    attend(last_z, 1 - core)
    take(twin_next)
    attend(next_z, 1 - core)
    twin_far = []
    for n, piece in enumerate(pieces):
        low_far[n].wait_recv()
        high_far[n].wait_recv()
        block = keys_values.at[far_z, core, piece]
        twin_far.append(copies.start(block, block, twin, keys_values.at[far_z, 1 - core, piece]))
    attend(far_z, core)
    take(twin_far)
    keep = pltpu.make_async_copy(keys_values, kv_all_ref, keep_sems.at[0])
    keep.start()
    attend(far_z, 1 - core)

    total_norm = norm[0:1, :]
    attended = (acc[...] / total_norm).T
    o_ref[...] = attended
    o_low[...] = attended.astype(bf16).reshape(4, ROWS, HD)
    lse_ref[...] = jnp.broadcast_to(top[0:1, :] + jnp.log2(total_norm), lse_ref.shape)
    q_all_ref[...] = queries[...]
    came_back = []
    for hop in HOPS:
        other = around(x, hop)
        came_back.append(
            copies.start(
                o_low.at[other],
                back.at[x],
                device(other, y, z, core),
                back.at[around(x, -hop)],
            )
        )
    back[x] = o_low[x]
    take(came_back)
    returned = jnp.concatenate([back[n] for n in range(4)], axis=1)
    returned_ref[...] = returned
    given[...] = dot(returned, out_weight_ref[...]).astype(bf16).reshape(given.shape)
    y_copies = Copies(y_send, y_recv)
    for step in sum_over_y(y_copies, here, given, came, all_rows):
        pass
    total_ref[...] = all_rows[...]
    copies.finish()
    y_copies.finish()
    keep.wait()


def attention_forward(q_heads, kv_heads, codes, bounds, out_weight):
    quarter = ROWS // SIDE
    width = out_weight.shape[1]
    whole = pl.BlockSpec(memory_space=pltpu.VMEM)
    count = 3 + 3 + 12 + 16 + 4 + 3
    outs = pl.pallas_call(
        forward_kernel,
        out_shape=[
            jax.ShapeDtypeStruct((4, ROWS, HD), bf16),
            jax.ShapeDtypeStruct((4, 2, 4, ROWS, 2 * HD), bf16),
            jax.ShapeDtypeStruct((4 * ROWS, HD), f32),
            jax.ShapeDtypeStruct((8, 4 * ROWS), f32),
            jax.ShapeDtypeStruct((ROWS, 4 * HD), bf16),
            jax.ShapeDtypeStruct((SIDE, quarter, width), bf16),
        ],
        in_specs=[whole] * 5,
        out_specs=[whole, pl.BlockSpec(memory_space=pl.ANY)] + [whole] * 4,
        scratch_shapes=[
            pltpu.VMEM((4, ROWS, HD), bf16),
            pltpu.VMEM((4, 2, 4, ROWS, 2 * HD), bf16),
            pltpu.VMEM((8, 4 * ROWS), f32),
            pltpu.VMEM((8, 4 * ROWS), f32),
            pltpu.VMEM((HD, 4 * ROWS), f32),
            pltpu.VMEM((4 * ROWS, HD), jnp.int32),
            pltpu.VMEM((4, ROWS, HD), bf16),
            pltpu.VMEM((4, ROWS, HD), bf16),
            pltpu.VMEM((SIDE, quarter, width), bf16),
            pltpu.VMEM((3, quarter, width), bf16),
            pltpu.VMEM((SIDE, quarter, width), bf16),
            pltpu.SemaphoreType.DMA((count,)),
            pltpu.SemaphoreType.DMA((count,)),
            pltpu.SemaphoreType.DMA((6,)),
            pltpu.SemaphoreType.DMA((6,)),
            pltpu.SemaphoreType.DMA((1,)),
        ],
        compiler_params=pltpu.CompilerParams(
            collective_id=0, has_side_effects=True, vmem_limit_bytes=VMEM_LIMIT
        ),
        name="attention_forward",
    )(q_heads, kv_heads, codes, bounds, out_weight)
    return list(outs[:5]) + [outs[5].reshape(ROWS, width)]


BACK_TILE = 256


def backward_kernel(
    grad_ref, q_ref, kv_hbm, o_ref, lse_ref, codes_ref, bounds_ref,
    packed_ref,
    keys_values, grads, delta, grad_q, grad_k, grad_v, column, parts, met, came, sums, q_low, back_q, back_kv,
    send_sems, recv_sems, load_sems,
):
    here = place()
    x, y, z, core = here
    twin = device(x, y, z, 1 - core)
    load = pltpu.make_async_copy(kv_hbm, keys_values, load_sems.at[0])
    load.start()
    meet(
        [device(around(x, hop), y, z, core) for hop in HOPS]
        + [device(x, y, around(z, hop), core) for hop in (1, 3)]
        + [twin]
    )
    copies = Copies(send_sems, recv_sems)
    arrivals = []
    for hop in HOPS:
        other = around(x, hop)
        arrivals.append(
            copies.start(
                grad_ref.at[other],
                grads.at[x],
                device(other, y, z, core),
                grads.at[around(x, -hop)],
            )
        )
    grads[x] = grad_ref[x]
    grad_q[...] = jnp.zeros_like(grad_q)
    load.wait()
    for arrival in arrivals:
        arrival.wait_recv()
    product = grads[...].reshape(4 * ROWS, HD).astype(f32) * o_ref[...]
    delta[...] = lax.dot_general(
        jnp.ones((8, HD), f32), product, NT, preferred_element_type=f32, precision=highest
    )

    def chunk(z_at, core_at):
        column[...] = key_column(codes_ref[z_at, core_at])
        grad_k[...] = jnp.zeros_like(grad_k)
        grad_v[...] = jnp.zeros_like(grad_v)

        def tile(index, carry):
            at = pl.ds(pl.multiple_of(index * BACK_TILE, BACK_TILE), BACK_TILE)
            query = q_ref[index]
            grad = grads[index]
            keys = keys_values[z_at, core_at, :, :, :HD].reshape(4 * ROWS, HD)
            values = keys_values[z_at, core_at, :, :, HD:].reshape(4 * ROWS, HD)
            scores = dot(keys, query, NT)
            codes = jnp.concatenate([column[...]] * (BACK_TILE // HD), axis=1)
            seen = visible(codes, bounds_ref[0:1, at], bounds_ref[1:2, at])
            weights = jnp.where(seen, jnp.exp2(scores - lse_ref[0:1, at]), 0.0)
            grad_weights = dot(values, grad, NT)
            grad_scores = (weights * (grad_weights - delta[0:1, at])).astype(bf16)
            grad_v[...] += dot(weights.astype(bf16), grad)
            grad_k[...] += dot(grad_scores, query)
            grad_q[:, at] += dot(keys, grad_scores, TN)
            return carry

        lax.fori_loop(0, 4 * ROWS // BACK_TILE, tile, 0)
        parts[z_at, core_at] = jnp.concatenate(
            [grad_k[...] * math.log(2.0), grad_v[...]], axis=1
        ).astype(bf16).reshape(2, 2 * ROWS, 2 * HD)

    def hand_over(z_at):
        return copies.start(
            parts.at[z_at, 1 - core], met.at[z_at], twin, met.at[z_at]
        )

    def join(z_at):
        parts[z_at, core] = (
            parts[z_at, core].astype(f32) + met[z_at].astype(f32)
        ).astype(bf16)

    next_z, last_z, far_z = around(z, 1), around(z, -1), around(z, 2)
    above, below = device(x, y, next_z, core), device(x, y, last_z, core)
    chunk(far_z, 1 - core)
    far_met = hand_over(far_z)
    chunk(far_z, core)
    chunk(next_z, 1 - core)
    next_met = hand_over(next_z)
    far_met.wait_recv()
    join(far_z)
    from_last = copies.start(parts.at[far_z, core, 0], came.at[0], above, came.at[0])
    from_next = copies.start(parts.at[far_z, core, 1], came.at[1], below, came.at[1])
    chunk(next_z, core)
    chunk(last_z, 1 - core)
    last_met = hand_over(last_z)
    next_met.wait_recv()
    join(next_z)
    raw_last = copies.start(parts.at[next_z, core, 1], came.at[2], above, came.at[2])
    chunk(last_z, core)
    chunk(z, 1 - core)
    own_met = hand_over(z)
    last_met.wait_recv()
    join(last_z)
    raw_next = copies.start(parts.at[last_z, core, 0], came.at[3], below, came.at[3])
    from_last.wait_recv()
    parts[next_z, core, 0] = (
        parts[next_z, core, 0].astype(f32) + came[0].astype(f32)
    ).astype(bf16)
    sum_last = copies.start(parts.at[next_z, core, 0], came.at[4], above, came.at[4])
    from_next.wait_recv()
    parts[last_z, core, 1] = (
        parts[last_z, core, 1].astype(f32) + came[1].astype(f32)
    ).astype(bf16)
    sum_next = copies.start(parts.at[last_z, core, 1], came.at[5], below, came.at[5])
    chunk(z, core)
    q_low[...] = (grad_q[...] * (HD**-0.5)).T.astype(bf16).reshape(4, ROWS, HD)
    arrivals = []
    for hop in HOPS:
        other = around(x, hop)
        arrivals.append(
            copies.start(
                q_low.at[other],
                back_q.at[x],
                device(other, y, z, core),
                back_q.at[around(x, -hop)],
            )
        )
    back_q[x] = q_low[x]
    own_met.wait_recv()
    raw_last.wait_recv()
    raw_next.wait_recv()
    sum_last.wait_recv()
    sum_next.wait_recv()
    mine = parts[z, core].astype(f32) + met[z].astype(f32)
    low = mine[0] + came[4].astype(f32) + came[3].astype(f32)
    high = mine[1] + came[2].astype(f32) + came[5].astype(f32)
    sums[0:2] = low.astype(bf16).reshape(2, ROWS, 2 * HD)
    sums[2:4] = high.astype(bf16).reshape(2, ROWS, 2 * HD)
    for hop in HOPS:
        other = around(x, hop)
        arrivals.append(
            copies.start(
                sums.at[other],
                back_kv.at[x],
                device(other, y, z, core),
                back_kv.at[around(x, -hop)],
            )
        )
    back_kv[x] = sums[x]
    for arrival in arrivals:
        arrival.wait_recv()
    for n in range(4):
        packed_ref[n, :, :HD] = back_q[n]
        packed_ref[n, :, HD:] = back_kv[n]
    copies.finish()


def attention_backward(grad_heads, q_all, kv_all, o_all, lse, codes, bounds):
    whole = pl.BlockSpec(memory_space=pltpu.VMEM)
    count = 3 + 4 + 6 + 6
    return pl.pallas_call(
        backward_kernel,
        out_shape=jax.ShapeDtypeStruct((4, ROWS, 3 * HD), bf16),
        in_specs=[whole, whole, pl.BlockSpec(memory_space=pl.ANY)] + [whole] * 4,
        out_specs=whole,
        scratch_shapes=[
            pltpu.VMEM((4, 2, 4, ROWS, 2 * HD), bf16),
            pltpu.VMEM((4, ROWS, HD), bf16),
            pltpu.VMEM((8, 4 * ROWS), f32),
            pltpu.VMEM((HD, 4 * ROWS), f32),
            pltpu.VMEM((4 * ROWS, HD), f32),
            pltpu.VMEM((4 * ROWS, HD), f32),
            pltpu.VMEM((4 * ROWS, HD), jnp.int32),
            pltpu.VMEM((4, 2, 2, 2 * ROWS, 2 * HD), bf16),
            pltpu.VMEM((4, 2, 2 * ROWS, 2 * HD), bf16),
            pltpu.VMEM((6, 2 * ROWS, 2 * HD), bf16),
            pltpu.VMEM((4, ROWS, 2 * HD), bf16),
            pltpu.VMEM((4, ROWS, HD), bf16),
            pltpu.VMEM((4, ROWS, HD), bf16),
            pltpu.VMEM((4, ROWS, 2 * HD), bf16),
            pltpu.SemaphoreType.DMA((count,)),
            pltpu.SemaphoreType.DMA((count,)),
            pltpu.SemaphoreType.DMA((1,)),
        ],
        compiler_params=pltpu.CompilerParams(
            collective_id=1, has_side_effects=True, vmem_limit_bytes=VMEM_LIMIT
        ),
        name="attention_backward",
    )(grad_heads, q_all, kv_all, o_all, lse, codes, bounds)


def layer_norm(values_in):
    row_mean = jnp.mean(values_in, axis=-1, keepdims=True)
    centred = values_in - row_mean
    inverse = lax.rsqrt(jnp.mean(centred * centred, axis=-1, keepdims=True) + 1e-05)
    return (centred * inverse, inverse)


def norm_back(grad_in, normed, inverse):
    return inverse * (
        grad_in
        - jnp.mean(grad_in, axis=-1, keepdims=True)
        - normed * jnp.mean(grad_in * normed, axis=-1, keepdims=True)
    )


def tables(place_now, head_dim):
    half_dim = head_dim // 2
    frequency = jnp.exp(
        jnp.arange(half_dim, dtype=jnp.float32) * (-2.0 * math.log(10000.0) / head_dim)
    )
    angles = place_now.astype(jnp.float32)[:, None] * frequency[None, :]
    angles = jnp.concatenate([angles, angles], axis=-1)
    return (jnp.cos(angles), jnp.sin(angles))


def rotate(values_in, cosine, sine):
    half_dim = values_in.shape[-1] // 2
    turned = jnp.concatenate([-values_in[..., half_dim:], values_in[..., :half_dim]], axis=-1)
    return values_in * cosine + turned * sine


def rotate_back(grad_in, cosine, sine):
    half_dim = grad_in.shape[-1] // 2
    scaled = grad_in * sine
    return grad_in * cosine + jnp.concatenate(
        [scaled[..., half_dim:], -scaled[..., :half_dim]], axis=-1
    )


def by_owner(factor):
    return factor.T.reshape(16, 2, factor.shape[1] // 32, ROWS)


def per_device(
    activations,
    labels,
    position,
    norm_gains,
    qkv_weight,
    out_weight,
    up_weight,
    down_weight,
    cotangent,
):
    mode_count = norm_gains.shape[0] // 2
    tok = lax.axis_index("tok")
    block, row = position // 256, position % 256
    second = (row >= 192).astype(jnp.int32)
    spot = jnp.where(second == 1, block * 64 + row - 192, block * 192 + row)
    code = spot + second * CLIP_STEP
    all_codes = lax.all_gather(code, "tok", axis=0)
    all_codes = all_codes.reshape(4, 4, 2, ROWS).transpose(1, 2, 0, 3).reshape(4, 2, 4 * ROWS)
    digits = jnp.stack([all_codes // 128, all_codes % 128], axis=2)
    codes = jnp.concatenate(
        [digits, jnp.zeros((4, 2, 6, 4 * ROWS), jnp.int32)], axis=2
    ).astype(bf16)
    own_codes = all_codes.reshape(8, 4 * ROWS)[tok % 8]
    own_low = jnp.where(own_codes >= CLIP_STEP, CLIP_STEP, 0)
    bounds = jnp.concatenate(
        [own_low[None], (own_codes - own_low)[None], jnp.zeros((6, 4 * ROWS), jnp.int32)], axis=0
    )

    residual = activations.astype(f32)
    onehot = (labels[:, None] == jnp.arange(mode_count, dtype=jnp.int32)[None, :]).astype(f32)
    gain_one = jnp.dot(onehot, norm_gains[:mode_count], precision=highest)
    gain_two = jnp.dot(onehot, norm_gains[mode_count:], precision=highest)
    normed_one, inverse_one = layer_norm(residual)
    input_one = (normed_one * gain_one).astype(bf16)
    cosine, sine = tables(spot, HD)
    projected = jnp.einsum("td,dkh->kth", input_one, qkv_weight, preferred_element_type=f32)
    projected = projected.reshape(3, ROWS, 4, HD).transpose(0, 2, 1, 3)
    q_heads = (rotate(projected[0], cosine, sine) * (HD**-0.5 / math.log(2.0))).astype(bf16)
    kv_heads = jnp.concatenate([rotate(projected[1], cosine, sine), projected[2]], axis=-1).astype(
        bf16
    )
    q_all, kv_all, o_all, lse, returned, attn_sum = attention_forward(
        q_heads, kv_heads, codes, bounds, out_weight
    )

    middle = residual + attn_sum.astype(f32)
    normed_two, inverse_two = layer_norm(middle)
    input_two = (normed_two * gain_two).astype(bf16)
    hidden = jnp.dot(input_two, up_weight, preferred_element_type=f32)
    grad_active = jnp.einsum("td,fd->tf", cotangent, down_weight, preferred_element_type=f32)
    active, gelu_pull = jax.vjp(
        lambda values_in: jax.nn.gelu(values_in, approximate=True), hidden
    )
    active = active.astype(bf16)
    grad_hidden = gelu_pull(grad_active)[0].astype(bf16)
    grad_two_part = jnp.einsum(
        "tf,df->td", grad_hidden, up_weight, preferred_element_type=f32
    ).astype(bf16)
    mlp_sum = lax.psum(
        jnp.dot(active, down_weight, preferred_element_type=f32).astype(bf16), "head"
    ).astype(f32)
    layer_out = (middle + mlp_sum).astype(bf16)

    grad_in_two, grad_down, grad_up = sum_and_grads(
        grad_two_part,
        [(by_owner(active), cotangent), (by_owner(input_two), grad_hidden)],
        2,
    )
    grad_in_two = grad_in_two.astype(f32)
    gain_two_grad = jnp.einsum("tm,td->md", onehot, grad_in_two * normed_two, precision=highest)
    grad_middle = cotangent.astype(f32) + norm_back(
        grad_in_two * gain_two, normed_two, inverse_two
    )
    grad_mid_low = grad_middle.astype(bf16)
    grad_heads = (
        jnp.einsum("td,ld->tl", grad_mid_low, out_weight, preferred_element_type=f32)
        .astype(bf16)
        .reshape(ROWS, 4, HD)
        .transpose(1, 0, 2)
    )
    packed = attention_backward(grad_heads, q_all, kv_all, o_all, lse, codes, bounds)

    packed_q = rotate_back(packed[:, :, :HD].astype(f32), cosine, sine).astype(bf16)
    packed_k = rotate_back(packed[:, :, HD : 2 * HD].astype(f32), cosine, sine).astype(bf16)
    grad_proj = (
        jnp.stack([packed_q, packed_k, packed[:, :, 2 * HD :]], axis=0)
        .transpose(2, 0, 1, 3)
        .reshape(ROWS, 3, 4 * HD)
    )
    grad_one_part = jnp.einsum(
        "tkh,dkh->td", grad_proj, qkv_weight, preferred_element_type=f32
    ).astype(bf16)
    grad_in_one, grad_qkv, grad_out = sum_and_grads(
        grad_one_part,
        [
            (by_owner(input_one), grad_proj.reshape(ROWS, 12 * HD)),
            (by_owner(returned), grad_mid_low),
        ],
        3,
    )
    grad_in_one = grad_in_one.astype(f32)
    gain_one_grad = jnp.einsum("tm,td->md", onehot, grad_in_one * normed_one, precision=highest)
    grad_input = grad_middle + norm_back(grad_in_one * gain_one, normed_one, inverse_one)
    gains_grad = jnp.concatenate([gain_one_grad, gain_two_grad], axis=0)
    gains_share = lax.psum_scatter(
        gains_grad.T.astype(bf16), "tok", scatter_dimension=0, tiled=True
    ).astype(f32)
    return (
        layer_out,
        grad_input,
        gains_share.T,
        grad_qkv.reshape(-1, 3, 4 * HD),
        grad_out,
        grad_up,
        grad_down,
    )


def solution(mesh):
    return jax.shard_map(
        per_device,
        mesh=mesh,
        in_specs=(
            P("tok", None),
            P("tok"),
            P("tok"),
            P(),
            P(None, None, "head"),
            P("head", None),
            P(None, "head"),
            P("head", None),
            P("tok", None),
        ),
        out_specs=(
            P("tok", None),
            P("tok", None),
            P(None, "tok"),
            P("tok", None, "head"),
            P(("head", "tok"), None),
            P("tok", "head"),
            P(("head", "tok"), None),
        ),
        check_vma=False,
    )
```

time: 1450 us -> 444 us (0.31)
  waiting for transfers between devices: 802 us -> 64.6 us
  local copies, waits for them, and re-layouts: 300 us -> 33.7 us
  Pallas kernels: 0 us -> 224 us
  matrix products: 169 us -> 46.4 us
  other arithmetic: 95.4 us -> 27.3 us
  starting transfers between devices: 39.7 us -> 0.37 us
    reduce_scatter x4 -> x0, waiting for transfers between devices: 351 us -> none  [the longest x1 94.4 us: per_device(): lax.psum_scatter(grad_down.astype(jnp.bfloat16), 'tok', scatter_dimension...]
    pallas_call x0 -> x4, Pallas kernels: none -> 224 us  [the longest x2 96.8 us: sum_and_grads(): pl.pallas_call(functools.partial(sum_kernel, shapes), out_shape=[jax.Shap...]
    unnamed x12 -> x3, waiting for transfers between devices: 234 us -> 64.6 us
    dot_general x17 -> x6, matrix products: 160 us -> 34.8 us  [the longest x1 7.68 us: per_device(): jnp.dot(active, down_weight, preferred_element_type=f32).astype(bf16)]
    psum x3 -> x1, waiting for transfers between devices: 117 us -> 0.01 us  [per_device(): lax.psum(jnp.dot(active, down_weight, preferred_element_type=f32).astype(...]
    slice x9 -> x0, local copies, waits for them, and re-layouts: 74.5 us -> none  [the longest x1 33.4 us: piece_scores(): value_heads = kv_piece[:, 1].reshape(key_count, heads_here, HD)]
    another operation x8 -> x2, local copies, waits for them, and re-layouts: 77.3 us -> 3.55 us  [the longest x1 2.59 us: per_device(): grad_proj.reshape(ROWS, 12 * HD)]
    all_gather x1 -> x0, waiting for transfers between devices: 65.1 us -> none  [over_keys(): lax.all_gather(keys_values, 'tok', axis=0, tiled=True)]
  transfers between devices with their start and end apart: 14 -> 2, of which waited for: 13 -> 1; matrix products, arithmetic and copies ran while one was open for 10% -> 3% of each run, Pallas kernels for 0% -> 0%
where the time goes in v1:
time: 444 us; the launch traced here: 438 us
  Pallas kernels  224 us (50%)
  waiting for transfers between devices  64.6 us (15%)
  matrix products  46.4 us (10%)
  local copies, waits for them, and re-layouts  33.7 us (8%)
  other arithmetic  27.3 us (6%)
  blocking collectives  25.6 us (6%)
  between operations  16.5 us (4%)
    pallas_call x2, Pallas kernels, sum_and_grads(): pl.pallas_call(functools.partial(sum_kernel, shapes), out_shape=[jax.Shap...  96.8 us
    pallas_call x1, Pallas kernels, attention_forward(): pl.pallas_call(forward_kernel, out_shape=[jax.ShapeDtypeStruct((4, ROWS,...  71.2 us
    unnamed x3, waiting for transfers between devices  64.6 us
    pallas_call x1, Pallas kernels, attention_backward(): pl.pallas_call(backward_kernel, out_shape=jax.ShapeDtypeStruct((4, ROWS,...  55.9 us
    all_gather x1, blocking collectives, per_device(): all_codes = lax.all_gather(code, 'tok', axis=0)  25.6 us
  transfers between devices with their start and end apart: 2, of which 1 were waited for; matrix products, arithmetic and copies ran while one was open for 3% of the time, Pallas kernels for 0%

profile of v1, /device:TPU:0, one launch (start us, length us, event | category | flops | bytes accessed | tf_op | source)
XLA Modules:
  0.0 438.2 jit_solution(6369426769838842004)
XLA Ops:
  11.3 2.5 fusion.6
  14.8 4.6 %convolution_bitcast_fusion.1 = f32[3,256,512]{2,1,0:T(8,128)S(1)} fusion(bf16[2048,3,512]{2,0,1:T(8,128)(2,1)} %param.13, bf16[256,2048]{1,0:T(8,128)(2,1)S(1)} %get-tuple-element.86), kind=kOutput, calls=%fused_computation.50 | convolution fusion | flops 1610612736 | bytes 8912896 | tf_op jit(solution)/shard_map/td,dkh->kth/dot_general | solution.py:807
  21.1 1.9 copy.37
  24.7 25.6 %all-gather.1 = s32[32,1,256]{2,1,0:T(1,128)S(1)} all-gather(s32[1,1,256]{2,1,0:T(1,128)S(1)} %bitcast.118), channel_id=2, replica_groups=mesh['tok'=32,'head'=4] {'tok'}, dimensions={0}, use_global_device_ids=true | all-gather | bytes 33792 | tf_op jit(solution)/shard_map/all_gather | solution.py:788
  57.7 71.2 %attention_forward.1 = (bf16[4,256,128]{2,1,0:T(8,128)(2,1)}, bf16[4,2,4,256,256]{4,3,2,1,0:T(8,128)(2,1)}, f32[1024,128]{1,0:T(8,128)}, f32[8,1024]{1,0:T(8,128...) custom-call(bf16[4,256,128]{2,1,0:T(8,128)(2,1)} %get-tuple-element.65.q_ref, ...), custom_call_target="tpu_custom_call" | custom-call | tf_op jit(solution)/shard_map/attention_forward/pallas_call | solution.py:502
  131.1 3.0 multiply_convert_fusion.1
  134.2 2.7 copy.41
  136.8 6.2 %fusion.68 = f32[256,2048]{1,0:T(8,128)S(1)} fusion(bf16[256,2048]{1,0:T(8,128)(2,1)} %refs_2_.1, bf16[2048,2048]{1,0:T(8,128)(2,1)} %param.16), kind=kOutput, calls=%fused_computation.142 | convolution fusion | flops 2147483648 | bytes 11534336 | tf_op jit(solution)/shard_map/td,fd->tf/dot_general | solution.py:821
  143.1 7.1 %fusion.18 = (bf16[256,2048]{1,0:T(8,128)(2,1)S(1)}, f32[256,2048]{1,0:T(8,128)S(1)}) fusion(f32[256,2048]{1,0:T(8,128)S(1)} %fusion.68, bf16[256,2048]{1,0:T(8,128)(2,1)S(1)} %copy-done.8, bf16[2048,2048]{1,0:T(8,128)(2,1)} %param.15), kind=kOutput, calls=%fused_computation.33 | convolution fusion | flops 2157969408 | bytes 14680064 | tf_op jit(solution)/shard_map/dot_general | solution.py:820
  150.2 3.3 convolution_convert_fusion
  155.2 2.4 copy.40
  157.7 55.9 %sum_and_grads_2.1 = (bf16[4,64,2048]{2,1,0:T(8,128)(2,1)}, f32[64,2048]{1,0:T(8,128)}, f32[64,2048]{1,0:T(8,128)}) custom-call(bf16[4,64,2048]{2,1,0:T(8,128)(2,1)} %bitcast.106, bf16[16,2,64,256]{3,2,1,0:T(8,128)(2,1)} %bitcast.101, bf16[256,2048]{1,0:T(8,128)(2,1)} %refs_2_.1, bf16[16,2,64,256]{3,2,1,0:T(8,128)(2,1)} %bitcast.100, ...), custom_call_target="tpu_custom_call" | custom-call | tf_op jit(solution)/shard_map/sum_and_grads_2/pallas_call | solution.py:299
  215.4 2.1 fusion.65
  223.5 55.9 %attention_backward.1 = bf16[4,256,384]{2,1,0:T(8,128)(2,1)} custom-call(bf16[4,256,128]{2,1,0:T(8,128)(2,1)} %bitcast.108, bf16[4,256,128]{2,1,0:T(8,128)(2,1)} %get-tuple-element.21.q_ref, bf16[4,2,4,256,256]{4,3,2,1,0:T(8,128)(2,1)} %get-tuple-element.22.kv_hbm, f32[1024,128]{1,0:T(8,128)} %get-tuple-element.23.o_ref, ...), custom_call_target="tpu_custom_call" | custom-call | tf_op jit(solution)/shard_map/attention_backward/pallas_call | solution.py:697
  285.5 2.4 copy.44
  287.9 2.3 copy.46
  291.0 2.2 convolution_convert_fusion.2
  293.1 2.6 reshape_reshape.7.refs_2_
  295.7 5.9 %fusion = bf16[256,2048]{1,0:T(8,128)(2,1)} fusion(bf16[256,3,512]{0,2,1:T(8,128)(2,1)} %bitcast.111, bf16[2048,3,512]{2,0,1:T(8,128)(2,1)} %param.13), kind=kOutput, calls=%fused_computation.11 | convolution fusion | flops 1611137024 | bytes 8126464 | tf_op jit(solution)/shard_map/tkh,dkh->td/dot_general | solution.py:861
  301.6 40.9 %sum_and_grads_3.1 = (bf16[4,64,2048]{2,1,0:T(8,128)(2,1)}, f32[64,1536]{1,0:T(8,128)}, f32[16,2048]{1,0:T(8,128)}) custom-call(bf16[4,64,2048]{2,1,0:T(8,128)(2,1)} %bitcast.110, bf16[16,2,64,256]{3,2,1,0:T(8,128)(2,1)} %bitcast.103, bf16[256,1536]{1,0:T(8,128)(2,1)} %reshape_reshape.7.refs_2_, bf16[16,2,16,256]{3,2,1,0:T(8,128)(2,1)} %bitcast.107, ...), custom_call_target="tpu_custom_call" | custom-call | tf_op jit(solution)/shard_map/sum_and_grads_3/pallas_call | solution.py:299
  342.5 2.4 convolution_convert_fusion.3
  346.4 7.7 %convolution_convert_fusion.1 = bf16[256,2048]{1,0:T(8,128)(2,1)} fusion(bf16[2048,2048]{1,0:T(8,128)(2,1)} %param.16, f32[256,2048]{1,0:T(8,128)} %copy-done.12), kind=kOutput, calls=%fused_computation.13 | convolution fusion | flops 2152726528 | bytes 11534336 | tf_op jit(solution)/shard_map/dot_general | solution.py:831
  356.7 64.6 %reduce-scatter.4.cloned.1.call-done = bf16[64,6]{1,0:T(8,128)(2,1)} async-done(((bf16[2048,6]{1,0:T(8,128)(2,1)}), bf16[64,6]{1,0:T(8,128)(2,1)}) %reduce-scatter.4.cloned.1.call-update) | async-done | bytes 784
  422.7 5.3 %fusion.10 = (f32[256,2048]{1,0:T(8,128)}, bf16[256,2048]{1,0:T(8,128)(2,1)}) fusion(f32[256,2048]{1,0:T(8,128)} %get-tuple-element.57, bf16[256,2048]{1,0:T(8,128)(2,1)S(1)} %copy-done, f32[256]{0:T(256)S(1)} %broadcast_multiply_fusion.1, f32[256]{0:T(256)S(1)} %broadcast_multiply_fusion.2, f32[256]{0:T(256)S(1)} %add_rsqrt_fusion.1, ...), kind=kLoop, calls=%fused_computation.25 | loop fusion | flops 7864320 | bytes 11538432 | tf_op jit(solution)/shard_map/add | solution.py:874
  (115 shorter events, 41.3 us)
Async XLA Ops:
  8.0 3.3 copy-start
  8.0 3.3 copy-start.21
  8.0 3.3 copy-start.18
  8.0 413.3 %reduce-scatter.4.cloned.1.call-start = ((), (), s32[]{:S(2)}) async-start(), calls=%async_computation.2 | async-start | bytes 540672
  22.9 1.7 copy-start.22
  54.3 1.1 copy-start.14
  128.9 1.7 copy-start.3
  136.8 6.2 %copy-start.8 = (bf16[256,2048]{1,0:T(8,128)(2,1)S(1)}, bf16[256,2048]{1,0:T(8,128)(2,1)}, u32[]{:S(2)}) copy-start(bf16[256,2048]{1,0:T(8,128)(2,1)} %get-tuple-element.58) | copy-start | bytes 3145732
  136.8 13.4 %slice-start = ((s8[8388608]{0:T(1024)(128)(4,1)}), s8[4194304]{0:T(1024)(128)(4,1)S(1)}, s32[]{:S(2)}) async-start(s8[8388608]{0:T(1024)(128)(4,1)} %bitcast.119), calls=%async_computation.3 | async-start | bytes 8388608
  143.1 7.2 %slice-start.1 = ((s8[8388608]{0:T(1024)(128)(4,1)}), s8[4194304]{0:T(1024)(128)(4,1)S(1)}, s32[]{:S(2)}) async-start(s8[8388608]{0:T(1024)(128)(4,1)} %bitcast.119), calls=%async_computation.4 | async-start | bytes 8388608
  150.2 3.4 copy-start.13
  150.2 3.4 copy-start.12
  157.6 55.9 %copy-start.1 = (f32[256,2048]{1,0:T(8,128)S(1)}, f32[256,2048]{1,0:T(8,128)}, u32[]{:S(2)}) copy-start(f32[256,2048]{1,0:T(8,128)} %get-tuple-element.88) | copy-start | bytes 6291460
  213.6 1.9 copy-start.4
  213.6 1.9 copy-start.9
  215.4 3.1 copy-start.11
  281.5 1.1 copy-start.6
  285.5 4.6 %copy-start.19 = (bf16[256,512]{1,0:T(8,128)(2,1)S(1)}, bf16[256,512]{1,0:T(8,128)(2,1)}, u32[]{:S(2)}) copy-start(bf16[256,512]{1,0:T(8,128)(2,1)} %get-tuple-element.25) | copy-start | bytes 786436
  346.0 8.1 %copy-start.17 = (f32[64,1536]{1,0:T(8,128)S(1)}, f32[64,1536]{1,0:T(8,128)}, u32[]{:S(2)}) copy-start(f32[64,1536]{1,0:T(8,128)} %get-tuple-element.27) | copy-start | bytes 1179652
  346.0 76.7 %all-reduce.2.cloned.1.call-start = ((), (), s32[]{:S(2)}) async-start(), calls=%async_computation.1 | async-start | bytes 2097152 | tf_op jit(solution)/shard_map/psum | solution.py:830
  346.4 8.5 %copy-start.2 = (f32[256,2048]{1,0:T(8,128)S(1)}, f32[256,2048]{1,0:T(8,128)}, u32[]{:S(2)}) copy-start(f32[256,2048]{1,0:T(8,128)} %get-tuple-element.87) | copy-start | bytes 6291460
  422.7 5.3 %copy-start.20 = (f32[16,2048]{1,0:T(8,128)S(1)}, f32[16,2048]{1,0:T(8,128)}, u32[]{:S(2)}) copy-start(f32[16,2048]{1,0:T(8,128)} %get-tuple-element.104) | copy-start | bytes 393220
  422.7 6.0 %copy-start.16 = (f32[64,2048]{1,0:T(8,128)S(1)}, f32[64,2048]{1,0:T(8,128)}, u32[]{:S(2)}) copy-start(f32[64,2048]{1,0:T(8,128)} %get-tuple-element.105) | copy-start | bytes 1572868
  422.7 6.8 %copy-start.15 = (f32[64,2048]{1,0:T(8,128)S(1)}, f32[64,2048]{1,0:T(8,128)}, u32[]{:S(2)}) copy-start(f32[64,2048]{1,0:T(8,128)} %get-tuple-element.106) | copy-start | bytes 1572868
  (3 other events, 2.9 us)
Sparse Core Ops, SparseCore 0:
  346.1 75.1 reduce-scatter.3
Sparse Core Ops, SparseCore 1:
  354.2 44.2 all-reduce.1

commit v2 on v1

--- a/solution.py
+++ b/solution.py
@@ -11,6 +11,7 @@
 HD = 128
 SIDE = 4
 ROWS = 256
+CODE_ROWS = 16
 CLIP_STEP = 8192
 MESH = pl.DeviceIdType.MESH
 NT = (((1,), (1,)), ((), ()))
@@ -109,6 +110,16 @@
     yield
 
 
+def sum_scratch(width):
+    quarter = ROWS // SIDE
+    return [
+        pltpu.VMEM((3, quarter, width), bf16),
+        pltpu.VMEM((SIDE, quarter, width), bf16),
+        pltpu.SemaphoreType.DMA((6,)),
+        pltpu.SemaphoreType.DMA((6,)),
+    ]
+
+
 def ring_sum(copies, own, towards, block, slots):
     up, down = towards(1), towards(-1)
     from_down = copies.start(block(2, 0), slots.at[0], up, slots.at[0])
@@ -152,21 +163,34 @@
     ]
 
 
-def weight_grad(here, left, right, out, scratch):
+def pick(core_at, factor, rows, group):
+    row = lax.broadcasted_iota(jnp.int32, (256, 512), 0)
+    col = lax.broadcasted_iota(jnp.int32, (256, 512), 1)
+    wanted = lax.div(row, rows) * (2 * rows) + core_at * rows + lax.rem(row, rows)
+    chosen = jnp.where(col == wanted, 1.0, 0.0).astype(bf16)
+    return dot(chosen, factor[:, 512 * group : 512 * (group + 1)], NT).astype(bf16)
+
+
+def weight_grad(here, left, right, out, scratch, far=None):
     both_left, both_right, parts, came, sums, late, send_sems, recv_sems, own_sems = scratch
     x, y, z, core = here
     rows, cols = out.shape
     half = cols // 4
     copies = Copies(send_sems, recv_sems)
     twin = device(x, y, z, 1 - core)
-    own_left = pltpu.make_async_copy(
-        left.at[:, core], both_left.at[:, :, pl.ds(0, ROWS)], own_sems.at[0]
-    )
-    own_right = pltpu.make_async_copy(right, both_right.at[pl.ds(0, ROWS)], own_sems.at[1])
-    own_left.start()
-    own_right.start()
+    if far is None:
+        far = left.at[:, 1 - core]
+        own_left = pltpu.make_async_copy(
+            left.at[:, core], both_left.at[:, :, pl.ds(0, ROWS)], own_sems.at[0]
+        )
+        own_right = pltpu.make_async_copy(right, both_right.at[pl.ds(0, ROWS)], own_sems.at[1])
+        own_left.start()
+        own_right.start()
+    else:
+        right = both_right.at[pl.ds(0, ROWS)]
+        own_left = own_right = None
     far_left = copies.start(
-        left.at[:, 1 - core],
+        far,
         both_left.at[:, :, pl.ds(ROWS, ROWS)],
         twin,
         both_left.at[:, :, pl.ds(ROWS, ROWS)],
@@ -178,8 +202,9 @@
         both_right.at[pl.ds(ROWS, ROWS)],
     )
     yield
-    own_left.wait()
-    own_right.wait()
+    if own_left is not None:
+        own_left.wait()
+        own_right.wait()
     far_left.wait_recv()
     far_right.wait_recv()
 
@@ -252,88 +277,185 @@
     yield
 
 
-def sum_kernel(shapes, *refs):
+def sum_gains(copies, here, given, came_x, part_x, came_z, part_z, came_core, part, came_y, out):
+    x, y, z, core = here
+    arrivals = [
+        copies.start(
+            given.at[around(x, hop)], came_x.at[n], device(around(x, hop), y, z, core), came_x.at[n]
+        )
+        for n, hop in enumerate(HOPS)
+    ]
+    yield
+    for arrival in arrivals:
+        arrival.wait_recv()
+    part_x[...] = (given[x] + came_x[0]) + (came_x[1] + came_x[2])
+    arrivals = [
+        copies.start(
+            part_x.at[around(z, hop)], came_z.at[n], device(x, y, around(z, hop), core), came_z.at[n]
+        )
+        for n, hop in enumerate(HOPS)
+    ]
+    yield
+    for arrival in arrivals:
+        arrival.wait_recv()
+    part_z[...] = (part_x[z] + came_z[0]) + (came_z[1] + came_z[2])
+    arrival = copies.start(part_z.at[1 - core], came_core, device(x, y, z, 1 - core), came_core)
+    yield
+    arrival.wait_recv()
+    part[...] = part_z[core] + came_core[...]
+    arrivals = [
+        copies.start(part, came_y.at[n], device(x, around(y, hop), z, core), came_y.at[n])
+        for n, hop in enumerate(HOPS)
+    ]
+    yield
+    for arrival in arrivals:
+        arrival.wait_recv()
+    out[...] = (part[...] + came_y[0]) + (came_y[1] + came_y[2])
+    yield
+
+
+GAIN_SCRATCH = [(3, 4, 2, 8, HD), (4, 2, 8, HD), (3, 2, 8, HD), (2, 8, HD), (8, HD), (8, HD), (3, 8, HD)]
+
+
+def sum_kernel(sum_count, shapes, with_gains, *refs):
+    refs = list(refs)
+
+    def take(count):
+        taken = refs[:count]
+        del refs[:count]
+        return taken
+
     count = len(shapes)
-    given = refs[0]
-    factors = refs[1 : 1 + 2 * count]
-    total = refs[1 + 2 * count]
-    outs = refs[2 + 2 * count : 2 + 3 * count]
-    came, all_rows, y_send, y_recv = refs[2 + 3 * count : 6 + 3 * count]
-    scratch = refs[6 + 3 * count :]
+    givens, factors, gains = take(sum_count), take(2 * count), take(int(with_gains))
+    totals, outs, gains_out = take(sum_count), take(count), take(int(with_gains))
+    sum_scratch = [take(4) for _ in range(sum_count)]
+    scratch = [take(9) for _ in range(count)]
     here = place()
     x, y, z, core = here
+    hops = HOPS if with_gains else (1, 3)
     meet(
         [device(x, around(y, hop), z, core) for hop in HOPS]
-        + [device(around(x, hop), y, z, core) for hop in (1, 3)]
-        + [device(x, y, around(z, hop), core) for hop in (1, 3)]
+        + [device(around(x, hop), y, z, core) for hop in hops]
+        + [device(x, y, around(z, hop), core) for hop in hops]
         + [device(x, y, z, 1 - core)]
     )
-    copies = Copies(y_send, y_recv)
-    over_y = sum_over_y(copies, here, given, came, all_rows)
+    over_y, y_copies = [], []
+    for given, (came, all_rows, y_send, y_recv) in zip(givens, sum_scratch):
+        y_copies.append(Copies(y_send, y_recv))
+        over_y.append(sum_over_y(y_copies[-1], here, given, came, all_rows))
     grads = [
-        weight_grad(here, factors[2 * n], factors[2 * n + 1], outs[n], scratch[9 * n : 9 * n + 9])
+        weight_grad(here, factors[2 * n], factors[2 * n + 1], outs[n], scratch[n])
         for n in range(count)
     ]
-    next(over_y)
+    over_all = iter(())
+    if with_gains:
+        gain_copies = Copies(refs[-2], refs[-1])
+        over_all = sum_gains(gain_copies, here, gains[0], *refs[: len(GAIN_SCRATCH)], gains_out[0])
+    next(over_y[0])
     for grad in grads:
         next(grad)
+    next(over_all, None)
     for grad in grads:
         next(grad)
-    next(over_y)
+    next(over_all, None)
+    next(over_y[0])
+    for later in over_y[1:]:
+        next(later)
     for grad in grads:
         next(grad)
-    next(over_y)
-    total[...] = all_rows[...]
-    copies.finish()
-    for step in range(3):
-        for grad in grads:
-            next(grad)
-
-
-def sum_and_grads(given, factors, collective_id):
+    next(over_all, None)
+    for later in over_y[1:]:
+        next(later)
+    next(over_y[0])
+    totals[0][...] = sum_scratch[0][1][...]
+    for grad in grads:
+        next(grad)
+    next(over_all, None)
+    for n in range(1, sum_count):
+        next(over_y[n])
+        totals[n][...] = sum_scratch[n][1][...]
+    for grad in grads:
+        next(grad)
+    next(over_all, None)
+    for grad in grads:
+        next(grad)
+    for copies in y_copies:
+        copies.finish()
+    if with_gains:
+        gain_copies.finish()
+
+
+def sum_and_grads(givens, factors, gains, collective_id):
     shapes = [(left.shape[2], right.shape[1]) for left, right in factors]
-    width = given.shape[1]
+    width = givens[0].shape[1]
     quarter = ROWS // SIDE
     flat = [array for pair in factors for array in pair]
     whole = pl.BlockSpec(memory_space=pltpu.VMEM)
+    sum_count = len(givens)
     outs = pl.pallas_call(
-        functools.partial(sum_kernel, shapes),
-        out_shape=[jax.ShapeDtypeStruct((SIDE, quarter, width), bf16)]
-        + [jax.ShapeDtypeStruct(shape, f32) for shape in shapes],
-        in_specs=[whole] + [pl.BlockSpec(memory_space=pl.ANY)] * len(flat),
-        out_specs=[whole] * (1 + len(shapes)),
+        functools.partial(sum_kernel, sum_count, shapes, gains is not None),
+        out_shape=[jax.ShapeDtypeStruct((SIDE, quarter, width), bf16)] * sum_count
+        + [jax.ShapeDtypeStruct(shape, f32) for shape in shapes]
+        + ([] if gains is None else [jax.ShapeDtypeStruct((8, HD), f32)]),
+        in_specs=[whole] * sum_count
+        + [pl.BlockSpec(memory_space=pl.ANY)] * len(flat)
+        + ([] if gains is None else [whole]),
+        out_specs=[whole] * (sum_count + len(shapes) + int(gains is not None)),
         scratch_shapes=[
             pltpu.VMEM((3, quarter, width), bf16),
             pltpu.VMEM((SIDE, quarter, width), bf16),
             pltpu.SemaphoreType.DMA((6,)),
             pltpu.SemaphoreType.DMA((6,)),
         ]
-        + [entry for shape in shapes for entry in weight_scratch(*shape)],
+        * sum_count
+        + [entry for shape in shapes for entry in weight_scratch(*shape)]
+        + (
+            []
+            if gains is None
+            else [pltpu.VMEM(shape, f32) for shape in GAIN_SCRATCH]
+            + [pltpu.SemaphoreType.DMA((10,)), pltpu.SemaphoreType.DMA((10,))]
+        ),
         compiler_params=pltpu.CompilerParams(
             collective_id=collective_id, has_side_effects=True, vmem_limit_bytes=VMEM_LIMIT
         ),
         name=f"sum_and_grads_{collective_id}",
-    )(given.reshape(SIDE, quarter, width), *flat)
-    return [outs[0].reshape(ROWS, width)] + list(outs[1:])
+    )(
+        *[given.reshape(SIDE, quarter, width) for given in givens],
+        *flat,
+        *([] if gains is None else [gains]),
+    )
+    return [total.reshape(ROWS, width) for total in outs[:sum_count]] + list(outs[sum_count:])
 
 
 def visible(key_codes, low, span):
     return (key_codes - low).astype(jnp.uint32) <= span.astype(jnp.uint32)
 
 
-def key_column(codes):
-    row = lax.broadcasted_iota(jnp.int32, (8, HD), 0)
+def key_column(keys_values, z_at, core_at):
+    codes = jnp.concatenate(
+        [keys_values[z_at, core_at, n, ROWS:, :] for n in range(4)], axis=1
+    )
+    row = lax.broadcasted_iota(jnp.int32, (CODE_ROWS, HD), 0)
     weight = jnp.where(row == 0, 128.0, jnp.where(row == 1, 1.0, 0.0)).astype(bf16)
     return dot(codes, weight, TN).astype(jnp.int32)
 
 
+def query_bounds(keys_values, z, core, bounds):
+    for n in range(4):
+        digits = keys_values[z, core, n, ROWS:, :].astype(f32)
+        code = (digits[0:1] * 128.0 + digits[1:2]).astype(jnp.int32)
+        low = jnp.where(code >= CLIP_STEP, CLIP_STEP, 0)
+        bounds[0:1, n * ROWS : (n + 1) * ROWS] = low
+        bounds[1:2, n * ROWS : (n + 1) * ROWS] = code - low
+
+
 QUERY_TILE = 512
 
 
 def forward_kernel(
-    q_ref, kv_ref, codes_ref, bounds_ref, out_weight_ref,
+    q_ref, kv_ref, out_weight_ref,
     q_all_ref, kv_all_ref, o_ref, lse_ref, returned_ref, total_ref,
-    queries, keys_values, top, norm, acc, column, o_low, back, given, came, all_rows,
+    queries, keys_values, top, norm, acc, column, bounds_ref, o_low, back, given, came, all_rows,
     send_sems, recv_sems, y_send, y_recv, keep_sems,
 ):
     here = place()
@@ -382,15 +504,16 @@
         from_twin.append(copies.start(block, block, twin, keys_values.at[z, 1 - core, piece]))
     for arrival in q_came:
         arrival.wait_recv()
+    query_bounds(keys_values, z, core, bounds_ref)
 
     def attend(z_at, core_at):
-        column[...] = key_column(codes_ref[z_at, core_at])
+        column[...] = key_column(keys_values, z_at, core_at)
 
         def tile(index, carry):
             at = pl.ds(pl.multiple_of(index * QUERY_TILE, QUERY_TILE), QUERY_TILE)
             query = queries[pl.ds(index * 2, 2)].reshape(QUERY_TILE, HD)
-            keys = keys_values[z_at, core_at, :, :, :HD].reshape(4 * ROWS, HD)
-            values = keys_values[z_at, core_at, :, :, HD:].reshape(4 * ROWS, HD)
+            keys = keys_values[z_at, core_at, :, :ROWS, :HD].reshape(4 * ROWS, HD)
+            values = keys_values[z_at, core_at, :, :ROWS, HD:].reshape(4 * ROWS, HD)
             scores = dot(keys, query, NT)
             codes = jnp.concatenate([column[...]] * (QUERY_TILE // HD), axis=1)
             seen = visible(codes, bounds_ref[0:1, at], bounds_ref[1:2, at])
@@ -421,13 +544,13 @@
         )
         from_next[n].wait_recv()
         block = keys_values.at[next_z, core, piece]
-        high = block.at[pl.ds(ROWS // 2, ROWS // 2)]
+        high = block.at[pl.ds(ROWS // 2, ROWS // 2 + CODE_ROWS)]
         high_far.append(
             copies.start(
                 high,
                 high,
                 below,
-                keys_values.at[far_z, core, piece, pl.ds(ROWS // 2, ROWS // 2)],
+                keys_values.at[far_z, core, piece, pl.ds(ROWS // 2, ROWS // 2 + CODE_ROWS)],
             )
         )
         twin_next.append(
@@ -494,7 +617,7 @@
     keep.wait()
 
 
-def attention_forward(q_heads, kv_heads, codes, bounds, out_weight):
+def attention_forward(q_heads, kv_heads, out_weight):
     quarter = ROWS // SIDE
     width = out_weight.shape[1]
     whole = pl.BlockSpec(memory_space=pltpu.VMEM)
@@ -503,21 +626,22 @@
         forward_kernel,
         out_shape=[
             jax.ShapeDtypeStruct((4, ROWS, HD), bf16),
-            jax.ShapeDtypeStruct((4, 2, 4, ROWS, 2 * HD), bf16),
+            jax.ShapeDtypeStruct((4, 2, 4, ROWS + CODE_ROWS, 2 * HD), bf16),
             jax.ShapeDtypeStruct((4 * ROWS, HD), f32),
             jax.ShapeDtypeStruct((8, 4 * ROWS), f32),
             jax.ShapeDtypeStruct((ROWS, 4 * HD), bf16),
             jax.ShapeDtypeStruct((SIDE, quarter, width), bf16),
         ],
-        in_specs=[whole] * 5,
+        in_specs=[whole] * 3,
         out_specs=[whole, pl.BlockSpec(memory_space=pl.ANY)] + [whole] * 4,
         scratch_shapes=[
             pltpu.VMEM((4, ROWS, HD), bf16),
-            pltpu.VMEM((4, 2, 4, ROWS, 2 * HD), bf16),
+            pltpu.VMEM((4, 2, 4, ROWS + CODE_ROWS, 2 * HD), bf16),
             pltpu.VMEM((8, 4 * ROWS), f32),
             pltpu.VMEM((8, 4 * ROWS), f32),
             pltpu.VMEM((HD, 4 * ROWS), f32),
             pltpu.VMEM((4 * ROWS, HD), jnp.int32),
+            pltpu.VMEM((8, 4 * ROWS), jnp.int32),
             pltpu.VMEM((4, ROWS, HD), bf16),
             pltpu.VMEM((4, ROWS, HD), bf16),
             pltpu.VMEM((SIDE, quarter, width), bf16),
@@ -533,18 +657,197 @@
             collective_id=0, has_side_effects=True, vmem_limit_bytes=VMEM_LIMIT
         ),
         name="attention_forward",
-    )(q_heads, kv_heads, codes, bounds, out_weight)
+    )(q_heads, kv_heads, out_weight)
     return list(outs[:5]) + [outs[5].reshape(ROWS, width)]
 
 
+NORM_ROWS = 32
+WIDE = 512
+
+
+def gain_rows(labels, gains, first):
+    return jnp.where(
+        labels == 0,
+        gains[first : first + 1, :],
+        jnp.where(labels == 1, gains[first + 1 : first + 2, :], gains[first + 2 : first + 3, :]),
+    )
+
+
+def gelu_and_slope(hidden):
+    scale = math.sqrt(2.0 / math.pi)
+    square = hidden * hidden
+    bent = jnp.tanh(scale * hidden * (1.0 + 0.044715 * square))
+    half = 0.5 * (1.0 + bent)
+    slope = half + 0.5 * hidden * (1.0 - bent * bent) * (scale * (1.0 + 3 * 0.044715 * square))
+    return hidden * half, slope
+
+
+def steps(count, body):
+    lax.fori_loop(0, count, lambda index, carry: (body(index), carry)[1], 0)
+
+
+def slab(index, size):
+    return pl.ds(pl.multiple_of(index * size, size), size)
+
+
+def middle_kernel(
+    x_ref, attn_ref, labels_ref, gains_ref, cotangent_ref, out_weight_ref, up_hbm, down_hbm,
+    g_mid_ref, g_low_ref, heads_ref, mlp_ref, active_left_ref, gains_out_ref, weight_ref,
+    up, down, xhat, inverse, normed, active, far, given, came, all_rows, y_send, y_recv, load_sems,
+    *weight_scratch_refs,
+):
+    here = place()
+    x, y, z, core = here
+    load_up = pltpu.make_async_copy(up_hbm, up, load_sems.at[0])
+    load_down = pltpu.make_async_copy(down_hbm, down, load_sems.at[1])
+    load_up.start()
+    load_down.start()
+    both_left, both_right = weight_scratch_refs[:2]
+    width = x_ref.shape[1]
+    hidden_width = up.shape[1]
+
+    def norm(index):
+        at = slab(index, NORM_ROWS)
+        middle = x_ref[at, :].astype(f32) + attn_ref[at, :].astype(f32)
+        centred = middle - jnp.mean(middle, axis=-1, keepdims=True)
+        scale = lax.rsqrt(jnp.mean(centred * centred, axis=-1, keepdims=True) + 1e-05)
+        unit = centred * scale
+        xhat[at, :] = unit
+        inverse[at, :] = jnp.broadcast_to(scale, (NORM_ROWS, HD))
+        normed[at, :] = (unit * gain_rows(labels_ref[at, :1], gains_ref, 3)).astype(bf16)
+
+    steps(ROWS // NORM_ROWS, norm)
+    load_up.wait()
+    load_down.wait()
+
+    def feed(index):
+        at = slab(index, WIDE)
+        hidden = dot(normed[...], up[:, at])
+        grad_active = dot(cotangent_ref[...], down[at, :], NT)
+        value, slope = gelu_and_slope(hidden)
+        active[:, at] = value.astype(bf16)
+        both_right[pl.ds(0, ROWS), at] = (grad_active * slope).astype(bf16)
+
+    steps(hidden_width // WIDE, feed)
+
+    def back_up(index):
+        at = slab(index, WIDE)
+        part = dot(both_right[pl.ds(0, ROWS), :], up[at, :], NT)
+        given[:, :, at] = part.astype(bf16).reshape(SIDE, ROWS // SIDE, WIDE)
+
+    steps(width // WIDE, back_up)
+    meet(
+        [device(x, around(y, hop), z, core) for hop in HOPS]
+        + [device(around(x, hop), y, z, core) for hop in (1, 3)]
+        + [device(x, y, around(z, hop), core) for hop in (1, 3)]
+        + [device(x, y, z, 1 - core)]
+    )
+    copies = Copies(y_send, y_recv)
+    over_y = sum_over_y(copies, here, given, came, all_rows)
+    next(over_y)
+    rows = weight_ref.shape[0]
+    for group in range(4):
+        at = pl.ds(4 * group, 4)
+        both_left[at, :, pl.ds(0, ROWS)] = pick(core, normed, rows, group).reshape(4, rows, ROWS)
+        far[at] = pick(1 - core, normed, rows, group).reshape(4, rows, ROWS)
+    ring = weight_grad(here, None, None, weight_ref, weight_scratch_refs, far)
+    next(ring)
+
+    def mlp(index):
+        at = slab(index, WIDE)
+        mlp_ref[:, :, at] = (
+            dot(active[...], down[:, at]).astype(bf16).reshape(SIDE, ROWS // SIDE, WIDE)
+        )
+
+    steps(width // WIDE, mlp)
+    next(ring)
+    for group in range(4):
+        for core_at in range(2):
+            active_left_ref[pl.ds(4 * group, 4), core_at] = pick(
+                core_at, active, rows, group
+            ).reshape(4, rows, ROWS)
+    next(over_y)
+    next(ring)
+    next(over_y)
+    gains_out_ref[...] = jnp.zeros_like(gains_out_ref)
+
+    def back(index):
+        at = slab(index, NORM_ROWS)
+        part = lax.div(index, SIDE // 2)
+        start = pl.multiple_of(lax.rem(index, SIDE // 2) * NORM_ROWS, NORM_ROWS)
+        grad = all_rows[part, pl.ds(start, NORM_ROWS), :].astype(f32)
+        labels = labels_ref[at, :1]
+        unit = xhat[at, :]
+        product = grad * unit
+        for mode in range(3):
+            gains_out_ref[mode : mode + 1, :] += jnp.sum(
+                jnp.where(labels == mode, product, 0.0), axis=0, keepdims=True
+            )
+        gain = gain_rows(labels, gains_ref, 3)
+        grad = grad * gain
+        mean = jnp.mean(grad, axis=-1, keepdims=True)
+        along = jnp.mean(product * gain, axis=-1, keepdims=True)
+        g_mid = cotangent_ref[at, :].astype(f32) + inverse[at, :1] * (grad - mean - unit * along)
+        g_mid_ref[at, :] = g_mid
+        g_low_ref[at, :] = g_mid.astype(bf16)
+
+    steps(ROWS // NORM_ROWS, back)
+    g_heads = dot(g_low_ref[...], out_weight_ref[...], NT).astype(bf16)
+    for head in range(4):
+        heads_ref[head] = g_heads[:, head * HD : (head + 1) * HD]
+    next(ring)
+    next(ring)
+    next(ring)
+    copies.finish()
+
+
+def middle(activations, attn_sum, labels, gains, cotangent, out_weight, up_weight, down_weight):
+    width, hidden_width = up_weight.shape
+    rows = width // 32
+    quarter = ROWS // SIDE
+    whole = pl.BlockSpec(memory_space=pltpu.VMEM)
+    anywhere = pl.BlockSpec(memory_space=pl.ANY)
+    return pl.pallas_call(
+        middle_kernel,
+        out_shape=[
+            jax.ShapeDtypeStruct((ROWS, width), f32),
+            jax.ShapeDtypeStruct((ROWS, width), bf16),
+            jax.ShapeDtypeStruct((4, ROWS, HD), bf16),
+            jax.ShapeDtypeStruct((SIDE, quarter, width), bf16),
+            jax.ShapeDtypeStruct((16, 2, hidden_width // 32, ROWS), bf16),
+            jax.ShapeDtypeStruct((8, width), f32),
+            jax.ShapeDtypeStruct((rows, hidden_width), f32),
+        ],
+        in_specs=[whole] * 6 + [anywhere] * 2,
+        out_specs=[whole] * 7,
+        scratch_shapes=[
+            pltpu.VMEM(up_weight.shape, bf16),
+            pltpu.VMEM(down_weight.shape, bf16),
+            pltpu.VMEM((ROWS, width), f32),
+            pltpu.VMEM((ROWS, HD), f32),
+            pltpu.VMEM((ROWS, width), bf16),
+            pltpu.VMEM((ROWS, hidden_width), bf16),
+            pltpu.VMEM((16, rows, ROWS), bf16),
+            pltpu.VMEM((SIDE, quarter, width), bf16),
+        ]
+        + sum_scratch(width)
+        + [pltpu.SemaphoreType.DMA((2,))]
+        + weight_scratch(rows, hidden_width),
+        compiler_params=pltpu.CompilerParams(
+            collective_id=2, has_side_effects=True, vmem_limit_bytes=VMEM_LIMIT
+        ),
+        name="middle",
+    )(activations, attn_sum, labels, gains, cotangent, out_weight, up_weight, down_weight)
+
+
 BACK_TILE = 256
 
 
 def backward_kernel(
-    grad_ref, q_ref, kv_hbm, o_ref, lse_ref, codes_ref, bounds_ref,
-    packed_ref,
-    keys_values, grads, delta, grad_q, grad_k, grad_v, column, parts, met, came, sums, q_low, back_q, back_kv,
-    send_sems, recv_sems, load_sems,
+    grad_ref, q_ref, kv_hbm, o_ref, lse_ref, left_ref, right_ref, given_ref,
+    packed_ref, weight_ref, total_ref,
+    keys_values, grads, delta, grad_q, grad_k, grad_v, column, bounds_ref, parts, met, came, sums, q_low, back_q,
+    back_kv, send_sems, recv_sems, load_sems, y_came, all_rows, y_send, y_recv, *weight_scratch_refs,
 ):
     here = place()
     x, y, z, core = here
@@ -553,10 +856,13 @@
     load.start()
     meet(
         [device(around(x, hop), y, z, core) for hop in HOPS]
+        + [device(x, around(y, hop), z, core) for hop in HOPS]
         + [device(x, y, around(z, hop), core) for hop in (1, 3)]
         + [twin]
     )
     copies = Copies(send_sems, recv_sems)
+    y_copies = Copies(y_send, y_recv)
+    over_y = sum_over_y(y_copies, here, given_ref, y_came, all_rows)
     arrivals = []
     for hop in HOPS:
         other = around(x, hop)
@@ -568,9 +874,14 @@
                 grads.at[around(x, -hop)],
             )
         )
+    ring = weight_grad(here, left_ref, right_ref, weight_ref, weight_scratch_refs)
+    next(ring)
     grads[x] = grad_ref[x]
     grad_q[...] = jnp.zeros_like(grad_q)
     load.wait()
+    query_bounds(keys_values, z, core, bounds_ref)
+    next(over_y)
+    next(ring)
     for arrival in arrivals:
         arrival.wait_recv()
     product = grads[...].reshape(4 * ROWS, HD).astype(f32) * o_ref[...]
@@ -579,7 +890,7 @@
     )
 
     def chunk(z_at, core_at):
-        column[...] = key_column(codes_ref[z_at, core_at])
+        column[...] = key_column(keys_values, z_at, core_at)
         grad_k[...] = jnp.zeros_like(grad_k)
         grad_v[...] = jnp.zeros_like(grad_v)
 
@@ -587,8 +898,8 @@
             at = pl.ds(pl.multiple_of(index * BACK_TILE, BACK_TILE), BACK_TILE)
             query = q_ref[index]
             grad = grads[index]
-            keys = keys_values[z_at, core_at, :, :, :HD].reshape(4 * ROWS, HD)
-            values = keys_values[z_at, core_at, :, :, HD:].reshape(4 * ROWS, HD)
+            keys = keys_values[z_at, core_at, :, :ROWS, :HD].reshape(4 * ROWS, HD)
+            values = keys_values[z_at, core_at, :, :ROWS, HD:].reshape(4 * ROWS, HD)
             scores = dot(keys, query, NT)
             codes = jnp.concatenate([column[...]] * (BACK_TILE // HD), axis=1)
             seen = visible(codes, bounds_ref[0:1, at], bounds_ref[1:2, at])
@@ -622,6 +933,8 @@
     chunk(far_z, core)
     chunk(next_z, 1 - core)
     next_met = hand_over(next_z)
+    next(ring)
+    next(over_y)
     far_met.wait_recv()
     join(far_z)
     from_last = copies.start(parts.at[far_z, core, 0], came.at[0], above, came.at[0])
@@ -629,12 +942,16 @@
     chunk(next_z, core)
     chunk(last_z, 1 - core)
     last_met = hand_over(last_z)
+    next(ring)
     next_met.wait_recv()
     join(next_z)
     raw_last = copies.start(parts.at[next_z, core, 1], came.at[2], above, came.at[2])
     chunk(last_z, core)
     chunk(z, 1 - core)
     own_met = hand_over(z)
+    next(ring)
+    next(over_y)
+    total_ref[...] = all_rows[...]
     last_met.wait_recv()
     join(last_z)
     raw_next = copies.start(parts.at[last_z, core, 0], came.at[3], below, came.at[3])
@@ -662,6 +979,7 @@
             )
         )
     back_q[x] = q_low[x]
+    next(ring)
     own_met.wait_recv()
     raw_last.wait_recv()
     raw_next.wait_recv()
@@ -689,24 +1007,31 @@
         packed_ref[n, :, :HD] = back_q[n]
         packed_ref[n, :, HD:] = back_kv[n]
     copies.finish()
-
-
-def attention_backward(grad_heads, q_all, kv_all, o_all, lse, codes, bounds):
+    y_copies.finish()
+
+
+def attention_backward(grad_heads, q_all, kv_all, o_all, lse, left, right, given):
     whole = pl.BlockSpec(memory_space=pltpu.VMEM)
+    anywhere = pl.BlockSpec(memory_space=pl.ANY)
     count = 3 + 4 + 6 + 6
     return pl.pallas_call(
         backward_kernel,
-        out_shape=jax.ShapeDtypeStruct((4, ROWS, 3 * HD), bf16),
-        in_specs=[whole, whole, pl.BlockSpec(memory_space=pl.ANY)] + [whole] * 4,
-        out_specs=whole,
+        out_shape=[
+            jax.ShapeDtypeStruct((4, ROWS, 3 * HD), bf16),
+            jax.ShapeDtypeStruct((left.shape[2], right.shape[1]), f32),
+            jax.ShapeDtypeStruct(given.shape, bf16),
+        ],
+        in_specs=[whole, whole, anywhere, whole, whole, anywhere, anywhere, whole],
+        out_specs=[whole, whole, whole],
         scratch_shapes=[
-            pltpu.VMEM((4, 2, 4, ROWS, 2 * HD), bf16),
+            pltpu.VMEM((4, 2, 4, ROWS + CODE_ROWS, 2 * HD), bf16),
             pltpu.VMEM((4, ROWS, HD), bf16),
             pltpu.VMEM((8, 4 * ROWS), f32),
             pltpu.VMEM((HD, 4 * ROWS), f32),
             pltpu.VMEM((4 * ROWS, HD), f32),
             pltpu.VMEM((4 * ROWS, HD), f32),
             pltpu.VMEM((4 * ROWS, HD), jnp.int32),
+            pltpu.VMEM((8, 4 * ROWS), jnp.int32),
             pltpu.VMEM((4, 2, 2, 2 * ROWS, 2 * HD), bf16),
             pltpu.VMEM((4, 2, 2 * ROWS, 2 * HD), bf16),
             pltpu.VMEM((6, 2 * ROWS, 2 * HD), bf16),
@@ -717,12 +1042,14 @@
             pltpu.SemaphoreType.DMA((count,)),
             pltpu.SemaphoreType.DMA((count,)),
             pltpu.SemaphoreType.DMA((1,)),
-        ],
+        ]
+        + sum_scratch(given.shape[2])
+        + weight_scratch(left.shape[2], right.shape[1]),
         compiler_params=pltpu.CompilerParams(
             collective_id=1, has_side_effects=True, vmem_limit_bytes=VMEM_LIMIT
         ),
         name="attention_backward",
-    )(grad_heads, q_all, kv_all, o_all, lse, codes, bounds)
+    )(grad_heads, q_all, kv_all, o_all, lse, left, right, given)
 
 
 def layer_norm(values_in):
@@ -780,27 +1107,18 @@
     cotangent,
 ):
     mode_count = norm_gains.shape[0] // 2
-    tok = lax.axis_index("tok")
     block, row = position // 256, position % 256
     second = (row >= 192).astype(jnp.int32)
     spot = jnp.where(second == 1, block * 64 + row - 192, block * 192 + row)
     code = spot + second * CLIP_STEP
-    all_codes = lax.all_gather(code, "tok", axis=0)
-    all_codes = all_codes.reshape(4, 4, 2, ROWS).transpose(1, 2, 0, 3).reshape(4, 2, 4 * ROWS)
-    digits = jnp.stack([all_codes // 128, all_codes % 128], axis=2)
-    codes = jnp.concatenate(
-        [digits, jnp.zeros((4, 2, 6, 4 * ROWS), jnp.int32)], axis=2
+    digits = jnp.stack([code // 128, code % 128], axis=0)
+    digits = jnp.concatenate(
+        [digits, jnp.zeros((CODE_ROWS - 2, ROWS), jnp.int32)], axis=0
     ).astype(bf16)
-    own_codes = all_codes.reshape(8, 4 * ROWS)[tok % 8]
-    own_low = jnp.where(own_codes >= CLIP_STEP, CLIP_STEP, 0)
-    bounds = jnp.concatenate(
-        [own_low[None], (own_codes - own_low)[None], jnp.zeros((6, 4 * ROWS), jnp.int32)], axis=0
-    )
 
     residual = activations.astype(f32)
     onehot = (labels[:, None] == jnp.arange(mode_count, dtype=jnp.int32)[None, :]).astype(f32)
     gain_one = jnp.dot(onehot, norm_gains[:mode_count], precision=highest)
-    gain_two = jnp.dot(onehot, norm_gains[mode_count:], precision=highest)
     normed_one, inverse_one = layer_norm(residual)
     input_one = (normed_one * gain_one).astype(bf16)
     cosine, sine = tables(spot, HD)
@@ -810,46 +1128,24 @@
     kv_heads = jnp.concatenate([rotate(projected[1], cosine, sine), projected[2]], axis=-1).astype(
         bf16
     )
+    kv_heads = jnp.concatenate(
+        [kv_heads, jnp.broadcast_to(digits[None], (4, CODE_ROWS, ROWS))], axis=1
+    )
     q_all, kv_all, o_all, lse, returned, attn_sum = attention_forward(
-        q_heads, kv_heads, codes, bounds, out_weight
-    )
-
-    middle = residual + attn_sum.astype(f32)
-    normed_two, inverse_two = layer_norm(middle)
-    input_two = (normed_two * gain_two).astype(bf16)
-    hidden = jnp.dot(input_two, up_weight, preferred_element_type=f32)
-    grad_active = jnp.einsum("td,fd->tf", cotangent, down_weight, preferred_element_type=f32)
-    active, gelu_pull = jax.vjp(
-        lambda values_in: jax.nn.gelu(values_in, approximate=True), hidden
-    )
-    active = active.astype(bf16)
-    grad_hidden = gelu_pull(grad_active)[0].astype(bf16)
-    grad_two_part = jnp.einsum(
-        "tf,df->td", grad_hidden, up_weight, preferred_element_type=f32
+        q_heads, kv_heads, out_weight
+    )
+
+    label_rows = jnp.broadcast_to(labels[:, None], (ROWS, HD))
+    gain_table = jnp.pad(norm_gains, ((0, 8 - 2 * mode_count), (0, 0)))
+    grad_middle, grad_mid_low, grad_heads, mlp_part, active_left, gain_two_grad, grad_up = middle(
+        activations, attn_sum, label_rows, gain_table, cotangent, out_weight, up_weight, down_weight
+    )
+    packed, grad_down, mlp_sum = attention_backward(
+        grad_heads, q_all, kv_all, o_all, lse, active_left, cotangent, mlp_part
+    )
+    layer_out = (
+        residual + attn_sum.astype(f32) + mlp_sum.reshape(ROWS, -1).astype(f32)
     ).astype(bf16)
-    mlp_sum = lax.psum(
-        jnp.dot(active, down_weight, preferred_element_type=f32).astype(bf16), "head"
-    ).astype(f32)
-    layer_out = (middle + mlp_sum).astype(bf16)
-
-    grad_in_two, grad_down, grad_up = sum_and_grads(
-        grad_two_part,
-        [(by_owner(active), cotangent), (by_owner(input_two), grad_hidden)],
-        2,
-    )
-    grad_in_two = grad_in_two.astype(f32)
-    gain_two_grad = jnp.einsum("tm,td->md", onehot, grad_in_two * normed_two, precision=highest)
-    grad_middle = cotangent.astype(f32) + norm_back(
-        grad_in_two * gain_two, normed_two, inverse_two
-    )
-    grad_mid_low = grad_middle.astype(bf16)
-    grad_heads = (
-        jnp.einsum("td,ld->tl", grad_mid_low, out_weight, preferred_element_type=f32)
-        .astype(bf16)
-        .reshape(ROWS, 4, HD)
-        .transpose(1, 0, 2)
-    )
-    packed = attention_backward(grad_heads, q_all, kv_all, o_all, lse, codes, bounds)
 
     packed_q = rotate_back(packed[:, :, :HD].astype(f32), cosine, sine).astype(bf16)
     packed_k = rotate_back(packed[:, :, HD : 2 * HD].astype(f32), cosine, sine).astype(bf16)
@@ -858,28 +1154,31 @@
         .transpose(2, 0, 1, 3)
         .reshape(ROWS, 3, 4 * HD)
     )
-    grad_one_part = jnp.einsum(
-        "tkh,dkh->td", grad_proj, qkv_weight, preferred_element_type=f32
-    ).astype(bf16)
-    grad_in_one, grad_qkv, grad_out = sum_and_grads(
-        grad_one_part,
+    grad_one_part = jnp.einsum("tkh,dkh->td", grad_proj, qkv_weight, preferred_element_type=f32)
+    gains_part = jnp.concatenate(
+        [
+            jnp.einsum("tm,td->md", onehot, grad_one_part * normed_one, precision=highest),
+            0.25 * gain_two_grad[:mode_count],
+        ],
+        axis=0,
+    )
+    gains_part = gains_part.reshape(2 * mode_count, 32, 64).transpose(1, 0, 2)
+    gains_part = jnp.pad(gains_part, ((0, 0), (0, 8 - 2 * mode_count), (0, HD - 64)))
+    grad_in_one, grad_qkv, grad_out, gains_share = sum_and_grads(
+        [grad_one_part.astype(bf16)],
         [
             (by_owner(input_one), grad_proj.reshape(ROWS, 12 * HD)),
             (by_owner(returned), grad_mid_low),
         ],
+        gains_part.reshape(4, 4, 2, 8, HD),
         3,
     )
     grad_in_one = grad_in_one.astype(f32)
-    gain_one_grad = jnp.einsum("tm,td->md", onehot, grad_in_one * normed_one, precision=highest)
     grad_input = grad_middle + norm_back(grad_in_one * gain_one, normed_one, inverse_one)
-    gains_grad = jnp.concatenate([gain_one_grad, gain_two_grad], axis=0)
-    gains_share = lax.psum_scatter(
-        gains_grad.T.astype(bf16), "tok", scatter_dimension=0, tiled=True
-    ).astype(f32)
     return (
         layer_out,
         grad_input,
-        gains_share.T,
+        gains_share[: 2 * mode_count, :64],
         grad_qkv.reshape(-1, 3, 4 * HD),
         grad_out,
         grad_up,

time: 444 us -> 294 us (0.66)
  waiting for transfers between devices: 64.6 us -> 0 us
  matrix products: 46.4 us -> 14 us
  blocking collectives: 25.6 us -> 0 us
  between operations: 16.5 us -> 1.18 us
  other arithmetic: 27.3 us -> 13.1 us
  Pallas kernels: 224 us -> 236 us
  local copies, waits for them, and re-layouts: 33.7 us -> 27.1 us
    unnamed x3 -> x0, waiting for transfers between devices: 64.6 us -> none
    dot_general x8 -> x1, matrix products: 33.4 us -> 1.13 us  [per_device(): jnp.einsum('tm,td->md', onehot, grad_one_part * normed_one, precision=hig...]
    all_gather x1 -> x0, blocking collectives: 25.6 us -> none  [per_device(): all_codes = lax.all_gather(code, 'tok', axis=0)]
    pallas_call x3, Pallas kernels: 153 us -> 163 us  [the longest x1 62.5 us: attention_backward(): pl.pallas_call(backward_kernel, out_shape=[jax.ShapeDtypeStruct((4, ROWS,...]
  transfers between devices with their start and end apart: 2 -> 0, of which waited for: 1 -> 0; matrix products, arithmetic and copies ran while one was open for 3% -> 0% of each run, Pallas kernels for 0% -> 0%
where the time goes in v2:
time: 294 us; the launch traced here: 291 us
  Pallas kernels  236 us (80%)
  local copies, waits for them, and re-layouts  27.1 us (9%)
  matrix products  14 us (5%)
  other arithmetic  13.1 us (4%)
    pallas_call x1, Pallas kernels, attention_forward(): pl.pallas_call(forward_kernel, out_shape=[jax.ShapeDtypeStruct((4, ROWS,...  72.9 us
    pallas_call x1, Pallas kernels, attention_backward(): pl.pallas_call(backward_kernel, out_shape=[jax.ShapeDtypeStruct((4, ROWS,...  62.5 us
    pallas_call x1, Pallas kernels, middle(): pl.pallas_call(middle_kernel, out_shape=[jax.ShapeDtypeStruct((ROWS, widt...  58.9 us
    pallas_call x1, Pallas kernels, sum_and_grads(): pl.pallas_call(functools.partial(sum_kernel, sum_count, shapes, gains is...  41.4 us
    dot_general x1, matrix products, per_device(): jnp.einsum('tkh,dkh->td', grad_proj, qkv_weight, preferred_element_type=f32)  5.94 us

profile of v2, /device:TPU:0, one launch (start us, length us, event | category | flops | bytes accessed | tf_op | source)
XLA Modules:
  0.0 291.1 jit_solution(15538815595839177758)
XLA Ops:
  0.8 1.5 convert_reduce_fusion
  2.3 1.6 fusion.13
  6.2 1.2 fusion.6
  7.4 1.5 copy.25
  8.9 5.7 %convolution_bitcast_fusion.1 = f32[3,256,512]{2,1,0:T(8,128)} fusion(bf16[2048,3,512]{2,0,1:T(8,128)(2,1)} %param.13, bf16[256,2048]{1,0:T(8,128)(2,1)S(1)} %get-tuple-element.86), kind=kOutput, calls=%fused_computation.20 | convolution fusion | flops 1610612736 | bytes 8912896 | tf_op jit(solution)/shard_map/td,dkh->kth/dot_general | solution.py:1125
  14.6 3.0 %copy.21 = f32[3,256,512]{1,2,0:T(8,128)} copy(f32[3,256,512]{2,1,0:T(8,128)} %convolution_bitcast_fusion.1) | data formatting | bytes 3145728 | tf_op jit(solution)/shard_map/td,dkh->kth/transpose | solution.py:1125
  17.6 3.0 %copy.22 = f32[3,256,4,128]{3,1,2,0:T(8,128)} copy(f32[3,256,4,128]{1,3,2,0:T(8,128)} %bitcast.62) | data formatting | bytes 3145728 | tf_op jit(solution)/shard_map/reshape | solution.py:1126
  20.6 1.1 fusion.29
  21.7 1.3 slice_bitcast_fusion
  24.4 1.1 fusion.28
  26.4 72.9 %attention_forward.1 = (bf16[4,256,128]{2,1,0:T(8,128)(2,1)}, bf16[4,2,4,272,256]{4,3,2,1,0:T(8,128)(2,1)}, f32[1024,128]{1,0:T(8,128)}, f32[8,1024]{1,0:T(8,128...) custom-call(bf16[4,256,128]{2,1,0:T(8,128)(2,1)} %get-tuple-element.67.q_ref, ...), custom_call_target="tpu_custom_call" | custom-call | tf_op jit(solution)/shard_map/attention_forward/pallas_call | solution.py:625
  99.2 1.8 copy.27
  101.0 58.9 %middle.1 = (f32[256,2048]{1,0:T(8,128)}, bf16[256,2048]{1,0:T(8,128)(2,1)}, bf16[4,256,128]{2,1,0:T(8,128)(2,1)}, bf16[4,64,2048]{2,1,0:T(8,128)(2,1)}, bf16[16...) custom-call(bf16[256,2048]{1,0:T(8,128)(2,1)} %x_ref.1, bf16[256,2048]{1,0:T(8,128)(2,1)} %bitcast.65, ...), custom_call_target="tpu_custom_call" | custom-call | tf_op jit(solution)/shard_map/middle/pallas_call | solution.py:810
  160.0 62.5 %attention_backward.1 = (bf16[4,256,384]{2,1,0:T(8,128)(2,1)}, f32[64,2048]{1,0:T(8,128)}, bf16[4,64,2048]{2,1,0:T(8,128)(2,1)}) custom-call(bf16[4,256,128]{2,1,0:T(8,128)(2,1)} %get-tuple-element.28.grad_ref, bf16[4,256,128]{2,1,0:T(8,128)(2,1)} %get-tuple-element.29.q_ref, bf16[4,2,4,272,256]{4,3,2,1,0:T(8,128)(2,1)} %get-tuple-element.30.kv_hbm, ...), custom_call_target="tpu_custom_call" | custom-call | tf_op jit(solution)/shard_map/attention_backward/pallas_call | solution.py:1017
  223.5 1.1 convert_multiply_fusion.3
  226.2 1.5 copy.26
  227.7 1.2 copy.23
  228.9 2.5 reshape_reshape.3.refs_2_
  231.4 5.9 %fusion.42 = (bf16[256,2048]{1,0:T(8,128)(2,1)}, f32[256,2048]{1,0:T(8,128)S(1)}) fusion(bf16[256,3,512]{0,2,1:T(8,128)(2,1)} %bitcast.68, bf16[2048,3,512]{2,0,1:T(8,128)(2,1)} %param.13), kind=kOutput, calls=%fused_computation.93 | convolution fusion | flops 1611137024 | bytes 10223616 | tf_op jit(solution)/shard_map/tkh,dkh->td/dot_general | solution.py:1157
  237.4 1.1 fusion.7
  239.4 41.4 %sum_and_grads_3.1 = (bf16[4,64,2048]{2,1,0:T(8,128)(2,1)}, f32[64,1536]{1,0:T(8,128)}, f32[16,2048]{1,0:T(8,128)}, f32[8,128]{1,0:T(8,128)}) custom-call(bf16[4,64,2048]{2,1,0:T(8,128)(2,1)} %bitcast.67, bf16[16,2,64,256]{3,2,1,0:T(8,128)(2,1)} %bitcast.63, bf16[256,1536]{1,0:T(8,128)(2,1)} %reshape_reshape.3.refs_2_, bf16[16,2,16,256]{3,2,1,0:T(8,128)(2,1)} %bitcast.66, ...), custom_call_target="tpu_custom_call" | custom-call | tf_op jit(solution)/shard_map/sum_and_grads_3/pallas_call | solution.py:395
  280.8 1.8 copy.34
  282.6 2.0 fusion.19
  285.1 2.9 %fusion.12 = (f32[256,2048]{1,0:T(8,128)}, bf16[256,2048]{1,0:T(8,128)(2,1)}) fusion(f32[256,2048]{1,0:T(8,128)S(1)} %copy-done.6, bf16[256,2048]{1,0:T(8,128)(2,1)S(1)} %copy-done.1, f32[256]{0:T(256)S(1)} %broadcast_multiply_fusion.1, f32[256]{0:T(256)S(1)} %broadcast_multiply_fusion.2, f32[256]{0:T(256)S(1)} %add_rsqrt_fusion, ...), kind=kLoop, calls=%fused_computation.15 | loop fusion | flops 7864320 | bytes 11538432 | tf_op jit(solution)/shard_map/add | solution.py:1177
  (66 shorter events, 11.3 us)
Async XLA Ops:
  0.6 5.5 %copy-start = (bf16[256,2048]{1,0:T(8,128)(2,1)S(1)}, bf16[256,2048]{1,0:T(8,128)(2,1)}, u32[]{:S(2)}) copy-start(bf16[256,2048]{1,0:T(8,128)(2,1)} %x_ref.1) | copy-start | bytes 3145732
  0.6 4.2 %copy-start.13 = (s32[256]{0:T(256)S(1)}, s32[256]{0:T(256)}, u32[]{:S(2)}) copy-start(s32[256]{0:T(256)} %param.10) | copy-start | bytes 3076
  0.7 3.5 %copy-start.10 = (f32[6,2048]{1,0:T(8,128)S(1)}, f32[6,2048]{1,0:T(8,128)}, u32[]{:S(2)}) copy-start(f32[6,2048]{1,0:T(8,128)} %param.12) | copy-start | bytes 147460
  0.7 3.3 %copy-start.15 = (s32[256]{0:T(256)S(1)}, s32[256]{0:T(256)}, u32[]{:S(2)}) copy-start(s32[256]{0:T(256)} %param.11) | copy-start | bytes 3076
  23.0 1.4 copy-start.2
  160.0 62.5 %copy-start.12 = (f32[8,2048]{1,0:T(8,128)S(1)}, f32[8,2048]{1,0:T(8,128)}, u32[]{:S(2)}) copy-start(f32[8,2048]{1,0:T(8,128)} %get-tuple-element.40) | copy-start | bytes 196612
  224.6 1.1 copy-start.5
  231.4 6.0 %copy-start.1 = (bf16[256,2048]{1,0:T(8,128)(2,1)S(1)}, bf16[256,2048]{1,0:T(8,128)(2,1)}, u32[]{:S(2)}) copy-start(bf16[256,2048]{1,0:T(8,128)(2,1)} %x_ref.1) | copy-start | bytes 3145732
  239.3 45.3 %copy-start.7 = (bf16[4,64,2048]{2,1,0:T(8,128)(2,1)S(1)}, bf16[4,64,2048]{2,1,0:T(8,128)(2,1)}, u32[]{:S(2)}) copy-start(bf16[4,64,2048]{2,1,0:T(8,128)(2,1)} %get-tuple-element.35) | copy-start | bytes 3145732
  282.6 2.0 copy-start.3
  282.6 2.0 copy-start.4
  282.6 2.5 copy-start.6
  285.1 2.9 %copy-start.14 = (f32[8,128]{1,0:T(8,128)S(1)}, f32[8,128]{1,0:T(8,128)}, u32[]{:S(2)}) copy-start(f32[8,128]{1,0:T(8,128)} %get-tuple-element.42) | copy-start | bytes 12292
  285.1 3.5 %copy-start.11 = (f32[16,2048]{1,0:T(8,128)S(1)}, f32[16,2048]{1,0:T(8,128)}, u32[]{:S(2)}) copy-start(f32[16,2048]{1,0:T(8,128)} %get-tuple-element.103) | copy-start | bytes 393220
  285.1 4.2 %copy-start.8 = (f32[64,2048]{1,0:T(8,128)S(1)}, f32[64,2048]{1,0:T(8,128)}, u32[]{:S(2)}) copy-start(f32[64,2048]{1,0:T(8,128)} %get-tuple-element.104) | copy-start | bytes 1572868
  285.1 5.0 %copy-start.9 = (f32[64,2048]{1,0:T(8,128)S(1)}, f32[64,2048]{1,0:T(8,128)}, u32[]{:S(2)}) copy-start(f32[64,2048]{1,0:T(8,128)} %get-tuple-element.105) | copy-start | bytes 1572868
